TPU v7x, 32 devices: a whole 2x2x4 slice. The times are simulated.
32 devices in a mesh: dp: 8 (over z, y), head: 4 (over x, core).
Axes of the slice: x: 2, y: 2, z: 4, core: 2. Of those that a mesh axis runs over, the one named last changes fastest.
Arguments:
- pixels: bfloat16 [4, 8, 512, 261], P(None, 'dp', 'head'), may hold values from -6 to 6
- masks: int32 [4, 8, 512], P(None, 'dp'), may hold values from 0 to 1, as said below
- valid: int32 [4, 8], P(None, 'dp'), may hold values 0 or 1
- labels: int32 [4, 8], P(None, 'dp'), may hold values from 0 to 999
- square: float32 [10, 1024, 1024], P(None, ('dp', 'head')), may hold values from -0.1875 to 0.1875
- kv_weight: float32 [261, 2048], P(None, ('dp', 'head')), may hold values from -0.375 to 0.375
- head_weight: float32 [1024, 1000], P(('dp', 'head')), may hold values from -0.375 to 0.375
- latents: float32 [512, 1024], P(None, ('dp', 'head')), may hold values from -6 to 6
- small: float32 [6381], replicated, may hold values from 0.25 to 1.75
- square_mom: float32 [10, 1024, 1024], P(None, ('dp', 'head')), may hold values from -0.005859375 to 0.005859375
- kv_mom: float32 [261, 2048], P(None, ('dp', 'head')), may hold values from -0.005859375 to 0.005859375
- head_mom: float32 [1024, 1000], P(('dp', 'head')), may hold values from -0.005859375 to 0.005859375
- latent_mom: float32 [512, 1024], P(None, ('dp', 'head')), may hold values from -6.1035156e-05 to 6.1035156e-05
- small_mom: float32 [6381], replicated, may hold values from -0.0625 to 0.0625
- square_avg: float32 [10, 1024, 1024], P(None, ('dp', 'head')), may hold values from -0.1875 to 0.1875
- kv_avg: float32 [261, 2048], P(None, ('dp', 'head')), may hold values from -0.375 to 0.375
- head_avg: float32 [1024, 1000], P(('dp', 'head')), may hold values from -0.1875 to 0.1875
- latent_avg: float32 [512, 1024], P(None, ('dp', 'head')), may hold values from -6 to 6
- small_avg: float32 [6381], replicated, may hold values from 0.25 to 1.75
Outputs:
- loss_sum: float32 [], replicated
- image_count: float32 [], replicated
- square_grad: float32 [10, 1024, 1024], P(None, ('dp', 'head'))
- square_mom_new: float32 [10, 1024, 1024], P(None, ('dp', 'head'))
- square_new: float32 [10, 1024, 1024], P(None, ('dp', 'head'))
- square_avg_new: float32 [10, 1024, 1024], P(None, ('dp', 'head'))
- kv_grad: float32 [261, 2048], P(None, ('dp', 'head'))
- kv_mom_new: float32 [261, 2048], P(None, ('dp', 'head'))
- kv_new: float32 [261, 2048], P(None, ('dp', 'head'))
- kv_avg_new: float32 [261, 2048], P(None, ('dp', 'head'))
- head_grad: float32 [1024, 1000], P(('dp', 'head'))
- head_mom_new: float32 [1024, 1000], P(('dp', 'head'))
- head_new: float32 [1024, 1000], P(('dp', 'head'))
- head_avg_new: float32 [1024, 1000], P(('dp', 'head'))
- latent_grad: float32 [512, 1024], P(None, ('dp', 'head'))
- latent_mom_new: float32 [512, 1024], P(None, ('dp', 'head'))
- latent_new: float32 [512, 1024], P(None, ('dp', 'head'))
- latent_avg_new: float32 [512, 1024], P(None, ('dp', 'head'))
- small_grad: float32 [6381], replicated
- small_mom_new: float32 [6381], replicated
- small_new: float32 [6381], replicated
- small_avg_new: float32 [6381], replicated
Inputs may be any that keep to these rules, and one draw needn't show every extreme that they name: `masks`: each image's mask is 1 on a leading run of at least 64 slots and 0 after it; in every micro-batch some image fills all 512 slots.
All inputs are finite; a program needn't handle non-finite values. No bound on the sum of `valid` on one device may be relied on, other than what follows from the above.
Results may differ from a plain program's by a relative error of at most 0.015.
Values may be sent and summed in bfloat16 or wider, within the bound.
A program may use at most 384 MiB of HBM per device.

v0:
```python
import math

import jax
import jax.numpy as jnp
from jax import lax
from jax.sharding import PartitionSpec as P

D = 1024
CIN = 261
LATENTS = 512
HEADS = 8
HEAD_DIM = 128
MICRO = 4
IMG_DEV = 1


EPS = 1e-05
NEG_BIG = -1e30
SMOOTH = 0.1
LEARN_RATE = 20.0
MOMENTUM = 0.9
AVERAGE_DECAY = 0.6


def layer_norm(v, gain):
    mean = jnp.mean(v, axis=-1, keepdims=True)
    cent = v - mean
    var = jnp.mean(cent * cent, axis=-1, keepdims=True)
    return cent * lax.rsqrt(var + EPS) * gain


def dot_nn(left, right):
    return jnp.dot(left, right, preferred_element_type=jnp.float32)


def dot_tn(left, right):
    return lax.dot_general(
        left, right, (((0,), (0,)), ((), ())), preferred_element_type=jnp.float32
    )


def dot_nt(left, right):
    return lax.dot_general(
        left, right, (((1,), (1,)), ((), ())), preferred_element_type=jnp.float32
    )


def scores_of(query, keys, valid_keys):
    scores = jnp.einsum("qhd,khd->hqk", query, keys, preferred_element_type=jnp.float32)
    scores = scores * query.shape[-1] ** (-0.5)
    if valid_keys is not None:
        scores = jnp.where(valid_keys[None, None, :], scores, NEG_BIG)
    return scores


def attend(query, keys, values, valid_keys):
    scores = scores_of(query, keys, valid_keys)
    log_total = jax.nn.logsumexp(scores, axis=-1, keepdims=True)
    probs = jnp.exp(scores - log_total).astype(jnp.bfloat16)
    out = jnp.einsum("hqk,khd->qhd", probs, values, preferred_element_type=jnp.float32)
    return (out.astype(jnp.bfloat16), log_total)


def attend_back(query, keys, values, log_total, d_out, valid_keys):
    scale = query.shape[-1] ** (-0.5)
    probs = jnp.exp(scores_of(query, keys, valid_keys) - log_total)
    probs_b = probs.astype(jnp.bfloat16)
    d_probs = jnp.einsum("qhd,khd->hqk", d_out, values, preferred_element_type=jnp.float32)
    d_scores = probs * (d_probs - jnp.sum(probs * d_probs, axis=-1, keepdims=True))
    d_scores = d_scores.astype(jnp.bfloat16)
    d_query = jnp.einsum("hqk,khd->qhd", d_scores, keys, preferred_element_type=jnp.float32) * scale
    d_keys = jnp.einsum("hqk,qhd->khd", d_scores, query, preferred_element_type=jnp.float32) * scale
    d_values = jnp.einsum("hqk,qhd->khd", probs_b, d_out, preferred_element_type=jnp.float32)
    return (d_query, d_keys, d_values)


def mlp_forward(hidden, gain, w_in, w_out):
    normed = layer_norm(hidden, gain).astype(jnp.bfloat16)
    pre = dot_nn(normed, w_in)
    active = jax.nn.gelu(pre).astype(jnp.bfloat16)
    return (hidden + dot_nn(active, w_out), (normed, pre, active))


def mlp_backward(hidden, gain, w_in, w_out, saved, d_next):
    normed, pre, active = saved
    d_next_b = d_next.astype(jnp.bfloat16)
    d_w_out = dot_tn(active, d_next_b)
    d_active = dot_nt(d_next_b, w_out)
    d_pre = jax.vjp(jax.nn.gelu, pre)[1](d_active)[0].astype(jnp.bfloat16)
    d_w_in = dot_tn(normed, d_pre)
    d_normed = dot_nt(d_pre, w_in)
    d_hidden, d_gain = jax.vjp(layer_norm, hidden, gain)[1](d_normed)
    return (d_next + d_hidden, d_gain, d_w_in, d_w_out)


def image_grads(weights, small, pixel_own, mask_row, valid_one, label, loss_scale, head_first):
    square, kv_weight, head_weight, latent_all, w_qkv = weights
    gains = small[: 5 * D].reshape(5, D)
    pix_gain = small[5 * D : 5 * D + CIN]
    bias = small[5 * D + CIN :]
    rows = latent_all.shape[0] // lax.axis_size("head")
    start = lax.axis_index("head") * rows
    latent_own = lax.dynamic_slice_in_dim(latent_all, start, rows, 0).astype(jnp.float32)
    valid_keys = mask_row > 0
    pix_float = pixel_own.astype(jnp.float32)
    normed_pix = layer_norm(pix_float, pix_gain).astype(jnp.bfloat16)
    kv_own = dot_nn(normed_pix, kv_weight).astype(jnp.bfloat16)
    kv_all = lax.all_gather(kv_own, "head", axis=0, tiled=True)
    keys_px = kv_all[:, :D].reshape(-1, 1, D)
    values_px = kv_all[:, D:].reshape(-1, 1, D)
    query_norm = layer_norm(latent_own, gains[0]).astype(jnp.bfloat16)
    query = dot_nn(query_norm, square[0]).astype(jnp.bfloat16).reshape(rows, 1, D)
    cross_out, cross_total = attend(query, keys_px, values_px, valid_keys)
    cross_out = cross_out.reshape(rows, D)
    hidden1 = latent_own + dot_nn(cross_out, square[1])
    hidden2, mlp_first = mlp_forward(hidden1, gains[1], square[2], square[3])
    self_norm = layer_norm(hidden2, gains[2]).astype(jnp.bfloat16)
    qkv = dot_nn(self_norm, w_qkv).astype(jnp.bfloat16)
    kv_latent = lax.all_gather(qkv[:, D:], "head", axis=0, tiled=True)
    self_query = qkv[:, :D].reshape(rows, HEADS, HEAD_DIM)
    self_keys = kv_latent[:, :D].reshape(-1, HEADS, HEAD_DIM)
    self_values = kv_latent[:, D:].reshape(-1, HEADS, HEAD_DIM)
    self_out, self_total = attend(self_query, self_keys, self_values, None)
    self_out = self_out.reshape(rows, D)
    hidden3 = hidden2 + dot_nn(self_out, square[7])
    hidden4, mlp_second = mlp_forward(hidden3, gains[3], square[8], square[9])
    final = layer_norm(hidden4, gains[4])
    pooled = lax.psum(jnp.sum(final, axis=0), "head") / latent_all.shape[0]
    pooled_b = pooled.astype(jnp.bfloat16)
    logits = dot_nn(pooled_b[None, :], head_weight)[0] + bias
    logp = jax.nn.log_softmax(logits)
    picked = jnp.arange(logits.shape[0]) == label
    loss = -valid_one * (
        (1.0 - SMOOTH) * jnp.sum(jnp.where(picked, logp, 0.0)) + SMOOTH * jnp.mean(logp)
    )
    target = (1.0 - SMOOTH) * picked.astype(jnp.float32) + SMOOTH / logits.shape[0]
    d_logits = valid_one * loss_scale * (jnp.exp(logp) - target)
    d_bias = d_logits * head_first
    d_head = pooled_b.astype(jnp.float32)[:, None] * d_logits[None, :] * head_first
    d_pooled = jnp.dot(head_weight.astype(jnp.float32), d_logits)
    d_final = jnp.broadcast_to(d_pooled / latent_all.shape[0], final.shape)
    d_hidden4, d_gain4 = jax.vjp(layer_norm, hidden4, gains[4])[1](d_final)
    d_hidden3, d_gain3, d_w8, d_w9 = mlp_backward(
        hidden3, gains[3], square[8], square[9], mlp_second, d_hidden4
    )
    d_hidden3_b = d_hidden3.astype(jnp.bfloat16)
    d_w7 = dot_tn(self_out, d_hidden3_b)
    d_self_out = dot_nt(d_hidden3_b, square[7]).astype(jnp.bfloat16).reshape(rows, HEADS, HEAD_DIM)
    d_query, d_keys, d_values = attend_back(
        self_query, self_keys, self_values, self_total, d_self_out, None
    )
    d_kv_terms = jnp.concatenate([d_keys.reshape(-1, D), d_values.reshape(-1, D)], axis=1)
    d_kv_own = lax.psum_scatter(
        d_kv_terms.astype(jnp.bfloat16), "head", scatter_dimension=0, tiled=True
    ).astype(jnp.float32)
    d_qkv = jnp.concatenate([d_query.reshape(rows, D), d_kv_own], axis=1).astype(jnp.bfloat16)
    d_w_qkv = dot_tn(self_norm, d_qkv)
    d_self_norm = dot_nt(d_qkv, w_qkv)
    d_hidden2_norm, d_gain2 = jax.vjp(layer_norm, hidden2, gains[2])[1](d_self_norm)
    d_hidden2 = d_hidden3 + d_hidden2_norm
    d_hidden1, d_gain1, d_w2, d_w3 = mlp_backward(
        hidden1, gains[1], square[2], square[3], mlp_first, d_hidden2
    )
    d_hidden1_b = d_hidden1.astype(jnp.bfloat16)
    d_w1 = dot_tn(cross_out, d_hidden1_b)
    d_cross = dot_nt(d_hidden1_b, square[1]).astype(jnp.bfloat16).reshape(rows, 1, D)
    d_query, d_keys, d_values = attend_back(
        query, keys_px, values_px, cross_total, d_cross, valid_keys
    )
    d_px_terms = jnp.concatenate([d_keys.reshape(-1, D), d_values.reshape(-1, D)], axis=1)
    d_kv_px = lax.psum_scatter(
        d_px_terms.astype(jnp.bfloat16), "head", scatter_dimension=0, tiled=True
    )
    d_kv_turned = dot_tn(d_kv_px, normed_pix)
    d_normed_pix = dot_nt(d_kv_px, kv_weight)
    d_pix_gain = jax.vjp(layer_norm, pix_float, pix_gain)[1](d_normed_pix)[1]
    d_query_b = d_query.reshape(rows, D).astype(jnp.bfloat16)
    d_w0 = dot_tn(query_norm, d_query_b)
    d_query_norm = dot_nt(d_query_b, square[0])
    d_latent_norm, d_gain0 = jax.vjp(layer_norm, latent_own, gains[0])[1](d_query_norm)
    d_latent_own = d_hidden1 + d_latent_norm
    d_square = jnp.stack(
        [
            d_w0,
            d_w1,
            d_w2,
            d_w3,
            d_w_qkv[:, :D],
            d_w_qkv[:, D : 2 * D],
            d_w_qkv[:, 2 * D :],
            d_w7,
            d_w8,
            d_w9,
        ]
    )
    latent_turned = lax.dynamic_update_slice_in_dim(
        jnp.zeros((D, latent_all.shape[0]), jnp.float32), d_latent_own.T, start, 1
    )
    d_small = jnp.concatenate(
        [jnp.stack([d_gain0, d_gain1, d_gain2, d_gain3, d_gain4]).reshape(-1), d_pix_gain, d_bias]
    )
    return ((d_square, d_kv_turned[None], d_head[None], latent_turned[None], d_small), loss)


def owner_layout(reduced):
    return (reduced[0], reduced[1][0].T, reduced[2][0], reduced[3][0].T)


def nesterov(weight, grad, mom, avg, rate):
    mom_new = MOMENTUM * mom + grad
    weight_new = weight - rate * (grad + MOMENTUM * mom_new)
    avg_new = AVERAGE_DECAY * avg + (1.0 - AVERAGE_DECAY) * weight_new
    return (grad, mom_new, weight_new, avg_new)


def per_device(
    pixels,
    masks,
    valid,
    labels,
    square,
    kv_weight,
    head_weight,
    latents,
    small,
    square_mom,
    kv_mom,
    head_mom,
    latent_mom,
    small_mom,
    square_avg,
    kv_avg,
    head_avg,
    latent_avg,
    small_avg,
):
    gathered = (
        lax.all_gather(square.astype(jnp.bfloat16), ("dp", "head"), axis=1, tiled=True),
        lax.all_gather(kv_weight.astype(jnp.bfloat16), ("dp", "head"), axis=1, tiled=True),
        lax.all_gather(head_weight.astype(jnp.bfloat16), ("dp", "head"), axis=0, tiled=True),
        lax.all_gather(latents.astype(jnp.bfloat16), ("dp", "head"), axis=1, tiled=True),
    )
    full_square = gathered[0]
    w_qkv = jnp.concatenate([full_square[4], full_square[5], full_square[6]], axis=1)
    weights = (full_square, gathered[1], gathered[2], gathered[3], w_qkv)
    head_first = (lax.axis_index("head") == 0).astype(jnp.float32)
    valid_float = valid.astype(jnp.float32)
    early_count = lax.psum(jnp.sum(valid_float), "dp")
    loss_scale = 1.0 / jnp.maximum(early_count, 1.0)
    kv_shape = gathered[1].shape
    lat_shape = gathered[3].shape
    big_zero = (
        jnp.zeros(full_square.shape, jnp.float32),
        jnp.zeros((1, kv_shape[1], kv_shape[0]), jnp.float32),
        jnp.zeros((1,) + gathered[2].shape, jnp.float32),
        jnp.zeros((1, lat_shape[1], lat_shape[0]), jnp.float32),
    )

    def micro_step(carry, batch):
        big, small_acc, loss_acc = carry
        pix_micro, mask_micro, valid_micro, label_micro = batch
        grads, loss_part = image_grads(
            weights,
            small,
            pix_micro[0],
            mask_micro[0],
            valid_micro[0],
            label_micro[0],
            loss_scale,
            head_first,
        )
        reduced = (grads[0], grads[1], grads[2], grads[3])
        big = tuple((a + b for a, b in zip(big, reduced)))
        return ((big, small_acc + grads[4], loss_acc + loss_part), None)

    start_carry = (big_zero, jnp.zeros(small.shape, jnp.float32), jnp.float32(0.0))
    (big, small_acc, loss_acc), _ = lax.scan(
        micro_step, start_carry, (pixels, masks, valid_float, labels)
    )
    big = owner_layout(
        (
            lax.psum_scatter(big[0], ("dp", "head"), scatter_dimension=1, tiled=True),
            lax.psum_scatter(big[1], ("dp", "head"), scatter_dimension=1, tiled=True),
            lax.psum_scatter(big[2], ("dp", "head"), scatter_dimension=1, tiled=True),
            lax.psum_scatter(big[3], ("dp", "head"), scatter_dimension=1, tiled=True),
        )
    )
    small_total, loss_sum, count = lax.psum(
        (small_acc, loss_acc * head_first, jnp.sum(valid_float) * head_first), ("dp", "head")
    )
    count = jnp.maximum(count, 1.0)
    latent_rate = LATENTS * math.sqrt(D * MICRO * IMG_DEV * lax.axis_size("dp")) / 32.0
    rates = (LEARN_RATE, LEARN_RATE, LEARN_RATE, latent_rate, LEARN_RATE)
    results = [loss_sum, count]
    params = (square, kv_weight, head_weight, latents, small)
    moms = (square_mom, kv_mom, head_mom, latent_mom, small_mom)
    avgs = (square_avg, kv_avg, head_avg, latent_avg, small_avg)
    for weight, grad, mom, avg, rate in zip(params, tuple(big) + (small_total,), moms, avgs, rates):
        results.extend(nesterov(weight, grad, mom, avg, rate))
    return tuple(results)


def solution(mesh):
    in_specs = (
        P(None, "dp", "head", None),
        P(None, "dp", None),
        P(None, "dp"),
        P(None, "dp"),
        P(None, ("dp", "head"), None),
        P(None, ("dp", "head")),
        P(("dp", "head"), None),
        P(None, ("dp", "head")),
        P(),
        P(None, ("dp", "head"), None),
        P(None, ("dp", "head")),
        P(("dp", "head"), None),
        P(None, ("dp", "head")),
        P(),
        P(None, ("dp", "head"), None),
        P(None, ("dp", "head")),
        P(("dp", "head"), None),
        P(None, ("dp", "head")),
        P(),
    )
    out_specs = (
        P(),
        P(),
        P(None, ("dp", "head"), None),
        P(None, ("dp", "head"), None),
        P(None, ("dp", "head"), None),
        P(None, ("dp", "head"), None),
        P(None, ("dp", "head")),
        P(None, ("dp", "head")),
        P(None, ("dp", "head")),
        P(None, ("dp", "head")),
        P(("dp", "head"), None),
        P(("dp", "head"), None),
        P(("dp", "head"), None),
        P(("dp", "head"), None),
        P(None, ("dp", "head")),
        P(None, ("dp", "head")),
        P(None, ("dp", "head")),
        P(None, ("dp", "head")),
        P(),
        P(),
        P(),
        P(),
    )
    return jax.shard_map(
        per_device, mesh=mesh, in_specs=in_specs, out_specs=out_specs, check_vma=False
    )
```

profile of v0, /device:TPU:0, one launch (start us, length us, event | category | flops | bytes accessed | tf_op | source)
XLA Modules:
  0.0 2174.6 jit_solution(12712614795307768385)
XLA Ops:
  13.3 23.8 %psum.39 = f32[]{:T(128)} all-reduce(f32[]{:T(128)} %convert_reduce_fusion.2), channel_id=1, replica_groups=mesh['dp'=8,'head'=4] {'dp'}, use_global_device_ids=true, to_apply=%region_1.0 | all-reduce | flops 1 | bytes 8 | tf_op jit(solution)/shard_map/psum | solution.py:248
  39.1 30.1 %all-gather.9.cloned.1.call-done = bf16[261,2048]{0,1:T(8,128)(2,1)} async-done(((bf16[261,64]{0,1:T(8,128)(2,1)}), bf16[261,2048]{0,1:T(8,128)(2,1)}) %all-gather.9.cloned.1.call-update) | async-done | bytes 1069072 | tf_op jit(solution)/shard_map/all_gather | solution.py:239
  70.8 134.6 %all-gather.11.cloned.1.call-done = bf16[10,1024,1024]{2,1,0:T(8,128)(2,1)} async-done(((bf16[10,32,1024]{2,1,0:T(8,128)(2,1)}), bf16[10,1024,1024]{2,1,0:T(8,128)(2,1)}) %all-gather.11.cloned.1.call-update) | async-done | bytes 20971536 | tf_op jit(solution)/shard_map/all_gather | solution.py:238
  212.2 48.8 %all-gather.7.cloned.1.call-done = bf16[512,1024]{0,1:T(8,128)(2,1)} async-done(((bf16[512,32]{0,1:T(8,128)(2,1)}), bf16[512,1024]{0,1:T(8,128)(2,1)}) %all-gather.7.cloned.1.call-update) | async-done | bytes 1048592 | tf_op jit(solution)/shard_map/all_gather | solution.py:241
  261.0 58.7 %all-gather.13.cloned.1.call-done = bf16[1024,1000]{1,0:T(8,128)(2,1)} async-done(((bf16[32,1000]{1,0:T(8,128)(2,1)}), bf16[1024,1000]{1,0:T(8,128)(2,1)}) %all-gather.13.cloned.1.call-update) | async-done | bytes 2048016 | tf_op jit(solution)/shard_map/all_gather | solution.py:240
  321.2 1013.3 %while.24 = (s32[]{:T(128)}, f32[10,1024,1024]{2,1,0:T(8,128)}, f32[1,2048,261]{1,2,0:T(8,128)}, f32[1,1024,1000]{2,1,0:T(8,128)}, f32[1,1024,512]{2,1,0:T(8,128...) while((s32[]{:T(128)}, f32[10,1024,1024]{2,1,0:T(8,128)}, ...), condition=%wide.region_45.46_spmd.clone, body=%wide.region_2.45_spmd.clone.sunk | while | flops 10166375424 | bytes 519892160 | solution.py:277
  352.8 17.2 all-gather.15.cloned.1.call-done
  386.6 18.7 all-gather.17.cloned.1.call-done
  420.2 5.9 psum.45
  465.0 22.9 %reduce-scatter.23.cloned.1.call-done = bf16[128,2048]{1,0:T(8,128)(2,1)} async-done(((bf16[512,2048]{1,0:T(8,128)(2,1)}), bf16[128,2048]{1,0:T(8,128)(2,1)}) %reduce-scatter.23.cloned.1.call-update) | async-done | bytes 524304 | tf_op jit(solution)/shard_map/while
  545.5 29.1 %select_add_fusion.6 = f32[10,1024,1024]{2,1,0:T(8,128)} fusion(f32[10,1024,1024]{2,1,0:T(8,128)} %bitcast_dynamic-update-slice_fusion.20, f32[10,1024,1024]{2,1,0:T(8,128)} %get-tuple-element.776, pred[]{:T(512)S(6)} %compare.3), kind=kLoop, calls=%fused_computation.clone.1 | loop fusion | flops 20971520 | bytes 125829120 | tf_op jit(solution)/shard_map/while/body/eval_jaxpr/add | solution.py:273
  588.3 18.5 all-gather.15.cloned.1.call-done
  623.4 18.7 all-gather.17.cloned.1.call-done
  657.0 5.9 psum.45
  704.4 20.2 reduce-scatter.23.cloned.1.call-done
  782.3 43.2 %select_add_fusion.6 = f32[10,1024,1024]{2,1,0:T(8,128)} fusion(f32[10,1024,1024]{2,1,0:T(8,128)} %bitcast_dynamic-update-slice_fusion.20, f32[10,1024,1024]{2,1,0:T(8,128)} %get-tuple-element.776, pred[]{:T(512)S(6)} %compare.3), kind=kLoop, calls=%fused_computation.clone.1 | loop fusion | flops 20971520 | bytes 125829120 | tf_op jit(solution)/shard_map/while/body/eval_jaxpr/add | solution.py:273
  839.1 18.5 all-gather.15.cloned.1.call-done
  874.2 18.7 all-gather.17.cloned.1.call-done
  907.8 5.9 psum.45
  950.0 5.2 select_add_fusion.7
  955.2 20.2 reduce-scatter.23.cloned.1.call-done
  1033.1 43.2 %select_add_fusion.6 = f32[10,1024,1024]{2,1,0:T(8,128)} fusion(f32[10,1024,1024]{2,1,0:T(8,128)} %bitcast_dynamic-update-slice_fusion.20, f32[10,1024,1024]{2,1,0:T(8,128)} %get-tuple-element.776, pred[]{:T(512)S(6)} %compare.3), kind=kLoop, calls=%fused_computation.clone.1 | loop fusion | flops 20971520 | bytes 125829120 | tf_op jit(solution)/shard_map/while/body/eval_jaxpr/add | solution.py:273
  1089.8 18.5 all-gather.15.cloned.1.call-done
  1125.0 18.7 all-gather.17.cloned.1.call-done
  1158.5 5.9 psum.45
  1206.0 20.2 reduce-scatter.23.cloned.1.call-done
  1283.9 43.2 %select_add_fusion.6 = f32[10,1024,1024]{2,1,0:T(8,128)} fusion(f32[10,1024,1024]{2,1,0:T(8,128)} %bitcast_dynamic-update-slice_fusion.20, f32[10,1024,1024]{2,1,0:T(8,128)} %get-tuple-element.776, pred[]{:T(512)S(6)} %compare.3), kind=kLoop, calls=%fused_computation.clone.1 | loop fusion | flops 20971520 | bytes 125829120 | tf_op jit(solution)/shard_map/while/body/eval_jaxpr/add | solution.py:273
  1340.9 40.4 %all-reduce = (f32[]{:T(128)}, f32[]{:T(128)}, f32[6381]{0:T(1024)}) all-reduce(f32[]{:T(128)S(6)} %mul.1102, f32[]{:T(128)S(6)} %mul.1103, f32[6381]{0:T(1024)S(1)} %copy-done.39), channel_id=1, replica_groups=mesh['dp'=8,'head'=4] {'dp','head'}, use_global_device_ids=true, to_apply=%region_46.47 | all-reduce | flops 6383 | bytes 51064 | tf_op jit(solution)/shard_map/psum | solution.py:288
  1383.4 59.7 %reduce-scatter.17.cloned.1.call-done = f32[1,64,261]{2,1,0:T(8,128)} async-done(((f32[1,2048,261]{2,1,0:T(8,128)}), f32[1,64,261]{2,1,0:T(8,128)}) %reduce-scatter.17.cloned.1.call-update) | async-done | bytes 66832 | tf_op jit(solution)/shard_map/reduce_scatter | solution.py:283
  1444.7 137.0 %reduce-scatter.21.cloned.1.call-done = f32[1,32,512]{2,1,0:T(8,128)} async-done(((f32[1,1024,512]{2,1,0:T(8,128)}), f32[1,32,512]{2,1,0:T(8,128)}) %reduce-scatter.21.cloned.1.call-update) | async-done | bytes 65552 | tf_op jit(solution)/shard_map/reduce_scatter | solution.py:285
  1583.3 138.2 %reduce-scatter.19.cloned.1.call-done = f32[1,32,1000]{2,1,0:T(8,128)} async-done(((f32[1,1024,1000]{2,1,0:T(8,128)}), f32[1,32,1000]{2,1,0:T(8,128)}) %reduce-scatter.19.cloned.1.call-update) | async-done | bytes 128016 | tf_op jit(solution)/shard_map/reduce_scatter | solution.py:284
  1723.2 439.0 %reduce-scatter.15.cloned.1.call-done = f32[10,32,1024]{2,1,0:T(8,128)} async-done(((f32[10,1024,1024]{2,1,0:T(8,128)}), f32[10,32,1024]{2,1,0:T(8,128)}) %reduce-scatter.15.cloned.1.call-update) | async-done | bytes 1310736 | tf_op jit(solution)/shard_map/reduce_scatter | solution.py:282
  (990 shorter events, 585.3 us)
Async XLA Ops:
  7.2 61.9 %all-gather.9.cloned.1.call-start = ((), (), s32[]{:S(2)}) async-start(), calls=%async_computation.7 | async-start | bytes 1622016 | tf_op jit(solution)/shard_map/all_gather | solution.py:239
  8.9 196.5 %all-gather.11.cloned.1.call-start = ((), (), s32[]{:S(2)}) async-start(), calls=%async_computation.8 | async-start | bytes 21626880 | tf_op jit(solution)/shard_map/all_gather | solution.py:238
  11.2 249.8 %all-gather.7.cloned.1.call-start = ((), (), s32[]{:S(2)}) async-start(), calls=%async_computation.6 | async-start | bytes 1081344 | tf_op jit(solution)/shard_map/all_gather | solution.py:241
  12.0 307.7 %all-gather.13.cloned.1.call-start = ((), (), s32[]{:S(2)}) async-start(), calls=%async_computation.9 | async-start | bytes 2162688 | tf_op jit(solution)/shard_map/all_gather | solution.py:240
  212.2 109.0 %copy-start.36 = (f32[6381]{0:T(1024)S(1)}, f32[6381]{0:T(1024)}, u32[]{:S(2)}) copy-start(f32[6381]{0:T(1024)} %param.29) | copy-start | bytes 76576
  344.1 25.9 %all-gather.15.cloned.1.call-start = ((), (), s32[]{:S(2)}) async-start(), calls=%async_computation.14 | async-start | bytes 2621440 | tf_op jit(solution)/shard_map/while/body/eval_jaxpr/all_gather | solution.py:108
  348.4 57.0 %all-gather.17.cloned.1.call-start = ((), (), s32[]{:S(2)}) async-start(), calls=%async_computation.15 | async-start | bytes 2621440 | tf_op jit(solution)/shard_map/while/body/eval_jaxpr/all_gather | solution.py:119
  382.6 105.2 %reduce-scatter.23.cloned.1.call-start = ((), (), s32[]{:S(2)}) async-start(), calls=%async_computation.16 | async-start | bytes 2621440 | tf_op jit(solution)/shard_map/while
  455.2 119.5 %reduce-scatter.25.cloned.1.call-start = ((), (), s32[]{:S(2)}) async-start(), calls=%async_computation.17 | async-start | bytes 2621440 | tf_op jit(solution)/shard_map/while
  579.7 27.1 %all-gather.15.cloned.1.call-start = ((), (), s32[]{:S(2)}) async-start(), calls=%async_computation.14 | async-start | bytes 2621440 | tf_op jit(solution)/shard_map/while/body/eval_jaxpr/all_gather | solution.py:108
  583.9 58.3 %all-gather.17.cloned.1.call-start = ((), (), s32[]{:S(2)}) async-start(), calls=%async_computation.15 | async-start | bytes 2621440 | tf_op jit(solution)/shard_map/while/body/eval_jaxpr/all_gather | solution.py:119
  619.4 105.2 %reduce-scatter.23.cloned.1.call-start = ((), (), s32[]{:S(2)}) async-start(), calls=%async_computation.16 | async-start | bytes 2621440 | tf_op jit(solution)/shard_map/while
  692.0 133.5 %reduce-scatter.25.cloned.1.call-start = ((), (), s32[]{:S(2)}) async-start(), calls=%async_computation.17 | async-start | bytes 2621440 | tf_op jit(solution)/shard_map/while
  830.4 27.1 %all-gather.15.cloned.1.call-start = ((), (), s32[]{:S(2)}) async-start(), calls=%async_computation.14 | async-start | bytes 2621440 | tf_op jit(solution)/shard_map/while/body/eval_jaxpr/all_gather | solution.py:108
  834.7 58.3 %all-gather.17.cloned.1.call-start = ((), (), s32[]{:S(2)}) async-start(), calls=%async_computation.15 | async-start | bytes 2621440 | tf_op jit(solution)/shard_map/while/body/eval_jaxpr/all_gather | solution.py:119
  870.2 105.2 %reduce-scatter.23.cloned.1.call-start = ((), (), s32[]{:S(2)}) async-start(), calls=%async_computation.16 | async-start | bytes 2621440 | tf_op jit(solution)/shard_map/while
  942.7 133.5 %reduce-scatter.25.cloned.1.call-start = ((), (), s32[]{:S(2)}) async-start(), calls=%async_computation.17 | async-start | bytes 2621440 | tf_op jit(solution)/shard_map/while
  1081.2 27.1 %all-gather.15.cloned.1.call-start = ((), (), s32[]{:S(2)}) async-start(), calls=%async_computation.14 | async-start | bytes 2621440 | tf_op jit(solution)/shard_map/while/body/eval_jaxpr/all_gather | solution.py:108
  1085.4 58.3 %all-gather.17.cloned.1.call-start = ((), (), s32[]{:S(2)}) async-start(), calls=%async_computation.15 | async-start | bytes 2621440 | tf_op jit(solution)/shard_map/while/body/eval_jaxpr/all_gather | solution.py:119
  1121.0 105.2 %reduce-scatter.23.cloned.1.call-start = ((), (), s32[]{:S(2)}) async-start(), calls=%async_computation.16 | async-start | bytes 2621440 | tf_op jit(solution)/shard_map/while
  1193.5 133.5 %reduce-scatter.25.cloned.1.call-start = ((), (), s32[]{:S(2)}) async-start(), calls=%async_computation.17 | async-start | bytes 2621440 | tf_op jit(solution)/shard_map/while
  1334.5 108.5 %reduce-scatter.17.cloned.1.call-start = ((), (), s32[]{:S(2)}) async-start(), calls=%async_computation.11 | async-start | bytes 3244032 | tf_op jit(solution)/shard_map/reduce_scatter | solution.py:283
  1337.9 243.8 %reduce-scatter.21.cloned.1.call-start = ((), (), s32[]{:S(2)}) async-start(), calls=%async_computation.13 | async-start | bytes 2162688 | tf_op jit(solution)/shard_map/reduce_scatter | solution.py:285
  1338.7 382.8 %reduce-scatter.19.cloned.1.call-start = ((), (), s32[]{:S(2)}) async-start(), calls=%async_computation.12 | async-start | bytes 4325376 | tf_op jit(solution)/shard_map/reduce_scatter | solution.py:284
  1339.4 822.8 %reduce-scatter.15.cloned.1.call-start = ((), (), s32[]{:S(2)}) async-start(), calls=%async_computation.10 | async-start | bytes 43253760 | tf_op jit(solution)/shard_map/reduce_scatter | solution.py:282
  1339.5 242.2 %copy-start.48 = (f32[512,32]{0,1:T(8,128)S(1)}, f32[512,32]{0,1:T(8,128)}, u32[]{:S(2)}) copy-start(f32[512,32]{0,1:T(8,128)} %param.28) | copy-start | bytes 196612
  1339.5 242.2 %copy-start.57 = (f32[512,32]{0,1:T(8,128)S(1)}, f32[512,32]{0,1:T(8,128)}, u32[]{:S(2)}) copy-start(f32[512,32]{0,1:T(8,128)} %param.38) | copy-start | bytes 196612
  1339.6 382.0 %copy-start.41 = (f32[32,1000]{1,0:T(8,128)S(1)}, f32[32,1000]{1,0:T(8,128)}, u32[]{:S(2)}) copy-start(f32[32,1000]{1,0:T(8,128)} %param.27) | copy-start | bytes 384004
  1339.6 382.0 %copy-start.51 = (f32[32,1000]{1,0:T(8,128)S(1)}, f32[32,1000]{1,0:T(8,128)}, u32[]{:S(2)}) copy-start(f32[32,1000]{1,0:T(8,128)} %param.37) | copy-start | bytes 384004
  1339.6 382.0 %copy-start.52 = (f32[32,1000]{1,0:T(8,128)S(1)}, f32[32,1000]{1,0:T(8,128)}, u32[]{:S(2)}) copy-start(f32[32,1000]{1,0:T(8,128)} %param.32) | copy-start | bytes 384004
  1339.6 822.6 %copy-start.35 = (f32[10,32,1024]{2,1,0:T(8,128)S(1)}, f32[10,32,1024]{2,1,0:T(8,128)}, u32[]{:S(2)}) copy-start(f32[10,32,1024]{2,1,0:T(8,128)} %param.35) | copy-start | bytes 3932164
  1340.0 822.2 %copy-start.34 = (f32[10,32,1024]{2,1,0:T(8,128)S(1)}, f32[10,32,1024]{2,1,0:T(8,128)}, u32[]{:S(2)}) copy-start(f32[10,32,1024]{2,1,0:T(8,128)} %param.25) | copy-start | bytes 3932164
  (197 other events, 2215.3 us)
Sparse Core Ops, SparseCore 0:
  11.5 57.6 all-gather.8
  72.7 132.6 all-gather.10
  208.8 52.1 all-gather.6
  264.3 55.3 all-gather.12
  348.5 21.4 all-gather.14
  382.7 22.6 all-gather.16
  455.3 32.4 reduce-scatter.22
  543.2 31.4 reduce-scatter.24
  584.0 22.7 all-gather.14
  619.5 22.5 all-gather.16
  692.1 32.4 reduce-scatter.22
  780.0 31.4 reduce-scatter.24
  834.8 22.7 all-gather.14
  870.3 22.5 all-gather.16
  942.9 32.4 reduce-scatter.22
  1030.8 31.4 reduce-scatter.24
  1085.6 22.7 all-gather.14
  1121.1 22.5 all-gather.16
  1193.6 32.4 reduce-scatter.22
  1281.6 31.4 reduce-scatter.24
  1341.4 101.6 reduce-scatter.16
  1445.9 135.8 reduce-scatter.20
  1584.7 136.8 reduce-scatter.18
  1724.4 437.7 reduce-scatter.14
where the time goes:
time: 2190 us; the launch traced here: 2170 us
  waiting for transfers between devices  1280 us (58%)
  matrix products  342 us (16%)
  other arithmetic  254 us (12%)
  local copies, waits for them, and re-layouts  150 us (7%)
  blocking collectives  87.8 us (4%)
  loops' own time  42.7 us (2%)
    reduce_scatter x1, waiting for transfers between devices, per_device(): lax.psum_scatter(big[0], ('dp', 'head'), scatter_dimension=1, tiled=True)  439 us
    add x8, other arithmetic, micro_step(): big = tuple((a + b for a, b in zip(big, reduced)))  177 us
    reduce_scatter x1, waiting for transfers between devices, per_device(): lax.psum_scatter(big[2], ('dp', 'head'), scatter_dimension=1, tiled=True)  138 us
    reduce_scatter x1, waiting for transfers between devices, per_device(): lax.psum_scatter(big[3], ('dp', 'head'), scatter_dimension=1, tiled=True)  137 us
    all_gather x1, waiting for transfers between devices, per_device(): lax.all_gather(square.astype(jnp.bfloat16), ('dp', 'head'), axis=1, tiled...  135 us
    dot_general x36, matrix products, dot_nt(): lax.dot_general(left, right, (((1,), (1,)), ((), ())), preferred_element_...  102 us
    dot_general x36, matrix products, dot_tn(): lax.dot_general(left, right, (((0,), (0,)), ((), ())), preferred_element_...  93 us
    dot_general x40, matrix products, dot_nn(): return jnp.dot(left, right, preferred_element_type=jnp.float32)  84 us
  transfers between devices with their start and end apart: 24, of which 21 were waited for; matrix products, arithmetic and copies ran while one was open for 12% of the time, Pallas kernels for 0%

commit v1 on v0

--- a/solution.py
+++ b/solution.py
@@ -213,7 +213,7 @@
     return (grad, mom_new, weight_new, avg_new)
 
 
-def per_device(
+def per_device_rows(
     pixels,
     masks,
     valid,
@@ -300,6 +300,148 @@
     return tuple(results)
 
 
+def image_forward_back(weights, small, pixels, mask_row, valid_one, label):
+    square, kv_weight, head_weight, latent_all = weights
+    gains = small[: 5 * D].reshape(5, D)
+    pix_gain = small[5 * D : 5 * D + CIN]
+    bias = small[5 * D + CIN :]
+    rows = latent_all.shape[0]
+    latent = latent_all.astype(jnp.float32)
+    valid_keys = mask_row > 0
+    pix_float = pixels.astype(jnp.float32)
+    normed_pix = layer_norm(pix_float, pix_gain).astype(jnp.bfloat16)
+    kv = dot_nn(normed_pix, kv_weight).astype(jnp.bfloat16)
+    keys_px = kv[:, :D].reshape(-1, 1, D)
+    values_px = kv[:, D:].reshape(-1, 1, D)
+    query_norm = layer_norm(latent, gains[0]).astype(jnp.bfloat16)
+    query = dot_nn(query_norm, square[0]).astype(jnp.bfloat16).reshape(rows, 1, D)
+    cross_out, cross_total = attend(query, keys_px, values_px, valid_keys)
+    cross_out = cross_out.reshape(rows, D)
+    hidden1 = latent + dot_nn(cross_out, square[1])
+    hidden2, mlp_first = mlp_forward(hidden1, gains[1], square[2], square[3])
+    self_norm = layer_norm(hidden2, gains[2]).astype(jnp.bfloat16)
+    qkv = [dot_nn(self_norm, square[i]).astype(jnp.bfloat16).reshape(rows, HEADS, HEAD_DIM) for i in (4, 5, 6)]
+    self_out, self_total = attend(qkv[0], qkv[1], qkv[2], None)
+    self_out = self_out.reshape(rows, D)
+    hidden3 = hidden2 + dot_nn(self_out, square[7])
+    hidden4, mlp_second = mlp_forward(hidden3, gains[3], square[8], square[9])
+    final = layer_norm(hidden4, gains[4])
+    pooled_b = (jnp.sum(final, axis=0) / rows).astype(jnp.bfloat16)
+    logits = dot_nn(pooled_b[None, :], head_weight)[0] + bias
+    logp = jax.nn.log_softmax(logits)
+    picked = jnp.arange(logits.shape[0]) == label
+    loss = -valid_one * (
+        (1.0 - SMOOTH) * jnp.sum(jnp.where(picked, logp, 0.0)) + SMOOTH * jnp.mean(logp)
+    )
+    target = (1.0 - SMOOTH) * picked.astype(jnp.float32) + SMOOTH / logits.shape[0]
+    d_logits = valid_one * (jnp.exp(logp) - target)
+    d_pooled = jnp.dot(head_weight.astype(jnp.float32), d_logits)
+    d_final = jnp.broadcast_to(d_pooled / rows, final.shape)
+    d_hidden4, d_gain4 = jax.vjp(layer_norm, hidden4, gains[4])[1](d_final)
+    d_hidden3, d_gain3, d_w8, d_w9 = mlp_backward(
+        hidden3, gains[3], square[8], square[9], mlp_second, d_hidden4
+    )
+    d_hidden3_b = d_hidden3.astype(jnp.bfloat16)
+    d_w7 = dot_tn(self_out, d_hidden3_b)
+    d_self_out = dot_nt(d_hidden3_b, square[7]).astype(jnp.bfloat16).reshape(rows, HEADS, HEAD_DIM)
+    d_parts = attend_back(qkv[0], qkv[1], qkv[2], self_total, d_self_out, None)
+    d_parts = [d.reshape(rows, D).astype(jnp.bfloat16) for d in d_parts]
+    d_w456 = [dot_tn(self_norm, d) for d in d_parts]
+    d_self_norm = sum(dot_nt(d, square[4 + i]) for i, d in enumerate(d_parts))
+    d_hidden2_norm, d_gain2 = jax.vjp(layer_norm, hidden2, gains[2])[1](d_self_norm)
+    d_hidden2 = d_hidden3 + d_hidden2_norm
+    d_hidden1, d_gain1, d_w2, d_w3 = mlp_backward(
+        hidden1, gains[1], square[2], square[3], mlp_first, d_hidden2
+    )
+    d_hidden1_b = d_hidden1.astype(jnp.bfloat16)
+    d_w1 = dot_tn(cross_out, d_hidden1_b)
+    d_cross = dot_nt(d_hidden1_b, square[1]).astype(jnp.bfloat16).reshape(rows, 1, D)
+    d_query, d_keys, d_values = attend_back(
+        query, keys_px, values_px, cross_total, d_cross, valid_keys
+    )
+    d_kv_px = jnp.concatenate([d_keys.reshape(-1, D), d_values.reshape(-1, D)], axis=1).astype(jnp.bfloat16)
+    d_kv_turned = dot_tn(d_kv_px, normed_pix)
+    d_normed_pix = dot_nt(d_kv_px, kv_weight)
+    d_pix_gain = jax.vjp(layer_norm, pix_float, pix_gain)[1](d_normed_pix)[1]
+    d_query_b = d_query.reshape(rows, D).astype(jnp.bfloat16)
+    d_w0 = dot_tn(query_norm, d_query_b)
+    d_query_norm = dot_nt(d_query_b, square[0])
+    d_latent_norm, d_gain0 = jax.vjp(layer_norm, latent, gains[0])[1](d_query_norm)
+    d_latent = d_hidden1 + d_latent_norm
+    d_square = [d_w0, d_w1, d_w2, d_w3] + d_w456 + [d_w7, d_w8, d_w9]
+    d_small = jnp.concatenate(
+        [d_gain0, d_gain1, d_gain2, d_gain3, d_gain4, d_pix_gain, d_logits]
+    )
+    return d_square, d_kv_turned, d_latent.T, d_small, pooled_b, d_logits, loss
+
+
+ALL = ("dp", "head")
+
+
+def gather_rows(shard):
+    return lax.all_gather(shard, ALL, axis=0, tiled=True)
+
+
+def scatter_rows(partial):
+    return lax.psum_scatter(partial.astype(jnp.bfloat16), ALL, scatter_dimension=0, tiled=True).astype(jnp.float32)
+
+
+def per_device_images(
+    pixels,
+    masks,
+    valid,
+    labels,
+    square,
+    kv_weight,
+    head_weight,
+    latents,
+    small,
+    square_mom,
+    kv_mom,
+    head_mom,
+    latent_mom,
+    small_mom,
+    square_avg,
+    kv_avg,
+    head_avg,
+    latent_avg,
+    small_avg,
+):
+    bf = jnp.bfloat16
+    micro = lax.axis_index("head")
+    pick = lambda a: lax.dynamic_index_in_dim(a, micro, 0, keepdims=False)[0]
+    image = lax.all_to_all(pixels[:, 0], "head", split_axis=0, concat_axis=1, tiled=True)[0]
+    latent_all = gather_rows(latents.astype(bf).T).T
+    kv_all = gather_rows(kv_weight.astype(bf).T).T
+    square_all = [gather_rows(square[i].astype(bf)) for i in range(10)]
+    head_all = gather_rows(head_weight.astype(bf))
+    valid_float = valid.astype(jnp.float32)
+    d_square, d_kv, d_lat, d_small, pooled_b, d_logits, loss = image_forward_back(
+        (square_all, kv_all, head_all, latent_all), small, image, pick(masks), pick(valid_float), pick(labels)
+    )
+    small_total, loss_sum, count = lax.psum((d_small, loss, pick(valid_float)), ALL)
+    count = jnp.maximum(count, 1.0)
+    pooled_all = lax.all_gather(pooled_b, ALL, axis=0)
+    logits_all = lax.all_gather(d_logits, ALL, axis=0)
+    own = head_weight.shape[0]
+    first = (lax.axis_index("dp") * lax.axis_size("head") + micro) * own
+    pooled_own = lax.dynamic_slice_in_dim(pooled_all, first, own, 1).astype(jnp.float32)
+    d_head = lax.dot_general(
+        pooled_own, logits_all, (((0,), (0,)), ((), ())), precision=lax.Precision.HIGHEST
+    )
+    d_square = jnp.stack([scatter_rows(d) for d in d_square])
+    grads = (d_square, scatter_rows(d_kv).T, d_head, scatter_rows(d_lat).T, small_total)
+    latent_rate = LATENTS * math.sqrt(D * MICRO * IMG_DEV * lax.axis_size("dp")) / 32.0
+    rates = (LEARN_RATE, LEARN_RATE, LEARN_RATE, latent_rate, LEARN_RATE)
+    results = [loss_sum, count]
+    params = (square, kv_weight, head_weight, latents, small)
+    moms = (square_mom, kv_mom, head_mom, latent_mom, small_mom)
+    avgs = (square_avg, kv_avg, head_avg, latent_avg, small_avg)
+    for weight, grad, mom, avg, rate in zip(params, grads, moms, avgs, rates):
+        results.extend(nesterov(weight, grad / count, mom, avg, rate))
+    return tuple(results)
+
+
 def solution(mesh):
     in_specs = (
         P(None, "dp", "head", None),
@@ -346,6 +488,8 @@
         P(),
         P(),
     )
+    whole_images = mesh.shape["head"] == MICRO
+    per_device = per_device_images if whole_images else per_device_rows
     return jax.shard_map(
         per_device, mesh=mesh, in_specs=in_specs, out_specs=out_specs, check_vma=False
     )

time: 2190 us -> 2570 us (1.17)
  waiting for transfers between devices: 1280 us -> 2200 us
  other arithmetic: 254 us -> 43.9 us
  matrix products: 342 us -> 149 us
  local copies, waits for them, and re-layouts: 150 us -> 54.5 us
  loops' own time: 42.7 us -> 0 us
    reduce_scatter x4 -> x12, waiting for transfers between devices: 774 us -> 1530 us  [scatter_rows(): lax.psum_scatter(partial.astype(jnp.bfloat16), ALL, scatter_dimension=0,...]
    all_gather x12 -> x13, waiting for transfers between devices: 420 us -> 662 us  [gather_rows(): return lax.all_gather(shard, ALL, axis=0, tiled=True)]
    add x16 -> x1, other arithmetic: 177 us -> 0.26 us  [image_forward_back(): d_hidden2 = d_hidden3 + d_hidden2_norm]
    while x24 -> x0, waiting for transfers between devices: 83.9 us -> none
    while x401 -> x0, local copies, waits for them, and re-layouts: 77 us -> none
    dot_general x36 -> x11, matrix products: 102 us -> 25.8 us  [dot_nt(): lax.dot_general(left, right, (((1,), (1,)), ((), ())), preferred_element_...]
    dot_general x36 -> x11, matrix products: 93 us -> 39 us  [dot_tn(): lax.dot_general(left, right, (((0,), (0,)), ((), ())), preferred_element_...]
    psum x6 -> x1, blocking collectives: 87.8 us -> 39.6 us  [per_device_images(): lax.psum((d_small, loss, pick(valid_float)), ALL)]
  transfers between devices with their start and end apart: 24 -> 27, of which waited for: 21 -> 26; matrix products, arithmetic and copies ran while one was open for 12% -> 6% of each run, Pallas kernels for 0% -> 0%
where the time goes in v1:
time: 2570 us; the launch traced here: 2560 us
  waiting for transfers between devices  2200 us (86%)
  matrix products  149 us (6%)
  blocking collectives  80.3 us (3%)
  local copies, waits for them, and re-layouts  54.5 us (2%)
  other arithmetic  43.9 us (2%)
    reduce_scatter x12, waiting for transfers between devices, scatter_rows(): lax.psum_scatter(partial.astype(jnp.bfloat16), ALL, scatter_dimension=0,...  1530 us
    all_gather x13, waiting for transfers between devices, gather_rows(): return lax.all_gather(shard, ALL, axis=0, tiled=True)  662 us
  transfers between devices with their start and end apart: 27, of which 26 were waited for; matrix products, arithmetic and copies ran while one was open for 6% of the time, Pallas kernels for 0%

profile of v1, /device:TPU:0, one launch (start us, length us, event | category | flops | bytes accessed | tf_op | source)
XLA Modules:
  0.0 2558.0 jit_solution(848546453720734053)
XLA Ops:
  30.1 37.7 %all-gather.26.cloned.1.call-done = bf16[1024,512]{1,0:T(8,128)(2,1)} async-done(((bf16[32,512]{1,0:T(8,128)(2,1)}), bf16[1024,512]{1,0:T(8,128)(2,1)}) %all-gather.26.cloned.1.call-update) | async-done | bytes 1048592 | tf_op jit(solution)/shard_map/all_gather | solution.py:382
  70.0 55.2 %all-gather.28.cloned.1.call-done = bf16[2048,261]{1,0:T(8,128)(2,1)} async-done(((bf16[64,261]{1,0:T(8,128)(2,1)}), bf16[2048,261]{1,0:T(8,128)(2,1)}) %all-gather.28.cloned.1.call-update) | async-done | bytes 1069072 | tf_op jit(solution)/shard_map/all_gather | solution.py:382
  129.4 54.6 %all-gather.32.cloned.1.call-done = bf16[1,1024,1024]{2,1,0:T(8,128)(2,1)} async-done(((bf16[1,32,1024]{2,1,0:T(8,128)(2,1)}), bf16[1,1024,1024]{2,1,0:T(8,128)(2,1)}) %all-gather.32.cloned.1.call-update) | async-done | bytes 2097168 | tf_op jit(solution)/shard_map/all_gather | solution.py:382
  190.7 51.8 %all-gather.34.cloned.1.call-done = bf16[1,1024,1024]{2,1,0:T(8,128)(2,1)} async-done(((bf16[1,32,1024]{2,1,0:T(8,128)(2,1)}), bf16[1,1024,1024]{2,1,0:T(8,128)(2,1)}) %all-gather.34.cloned.1.call-update) | async-done | bytes 2097168 | tf_op jit(solution)/shard_map/all_gather | solution.py:382
  247.5 53.6 %all-gather.36.cloned.1.call-done = bf16[1,1024,1024]{2,1,0:T(8,128)(2,1)} async-done(((bf16[1,32,1024]{2,1,0:T(8,128)(2,1)}), bf16[1,1024,1024]{2,1,0:T(8,128)(2,1)}) %all-gather.36.cloned.1.call-update) | async-done | bytes 2097168 | tf_op jit(solution)/shard_map/all_gather | solution.py:382
  305.3 54.3 %all-gather.38.cloned.1.call-done = bf16[1,1024,1024]{2,1,0:T(8,128)(2,1)} async-done(((bf16[1,32,1024]{2,1,0:T(8,128)(2,1)}), bf16[1,1024,1024]{2,1,0:T(8,128)(2,1)}) %all-gather.38.cloned.1.call-update) | async-done | bytes 2097168 | tf_op jit(solution)/shard_map/all_gather | solution.py:382
  359.6 5.7 fusion.159
  367.0 51.3 %all-gather.44.cloned.1.call-done = bf16[1,1024,1024]{2,1,0:T(8,128)(2,1)} async-done(((bf16[1,32,1024]{2,1,0:T(8,128)(2,1)}), bf16[1,1024,1024]{2,1,0:T(8,128)(2,1)}) %all-gather.44.cloned.1.call-update) | async-done | bytes 2097168 | tf_op jit(solution)/shard_map/all_gather | solution.py:382
  424.7 52.2 %all-gather.42.cloned.1.call-done = bf16[1,1024,1024]{2,1,0:T(8,128)(2,1)} async-done(((bf16[1,32,1024]{2,1,0:T(8,128)(2,1)}), bf16[1,1024,1024]{2,1,0:T(8,128)(2,1)}) %all-gather.42.cloned.1.call-update) | async-done | bytes 2097168 | tf_op jit(solution)/shard_map/all_gather | solution.py:382
  491.1 44.6 %all-gather.40.cloned.1.call-done = bf16[1,1024,1024]{2,1,0:T(8,128)(2,1)} async-done(((bf16[1,32,1024]{2,1,0:T(8,128)(2,1)}), bf16[1,1024,1024]{2,1,0:T(8,128)(2,1)}) %all-gather.40.cloned.1.call-update) | async-done | bytes 2097168 | tf_op jit(solution)/shard_map/all_gather | solution.py:382
  539.8 6.0 convolution_convert_fusion.13
  545.8 48.4 %all-gather.46.cloned.1.call-done = bf16[1,1024,1024]{2,1,0:T(8,128)(2,1)} async-done(((bf16[1,32,1024]{2,1,0:T(8,128)(2,1)}), bf16[1,1024,1024]{2,1,0:T(8,128)(2,1)}) %all-gather.46.cloned.1.call-update) | async-done | bytes 2097168 | tf_op jit(solution)/shard_map/all_gather | solution.py:382
  600.4 52.5 %all-gather.48.cloned.1.call-done = bf16[1,1024,1024]{2,1,0:T(8,128)(2,1)} async-done(((bf16[1,32,1024]{2,1,0:T(8,128)(2,1)}), bf16[1,1024,1024]{2,1,0:T(8,128)(2,1)}) %all-gather.48.cloned.1.call-update) | async-done | bytes 2097168 | tf_op jit(solution)/shard_map/all_gather | solution.py:382
  657.8 53.6 %all-gather.50.cloned.1.call-done = bf16[1,1024,1024]{2,1,0:T(8,128)(2,1)} async-done(((bf16[1,32,1024]{2,1,0:T(8,128)(2,1)}), bf16[1,1024,1024]{2,1,0:T(8,128)(2,1)}) %all-gather.50.cloned.1.call-update) | async-done | bytes 2097168 | tf_op jit(solution)/shard_map/all_gather | solution.py:382
  711.5 5.7 fusion.157
  718.5 51.6 %all-gather.30.cloned.1.call-done = bf16[1024,1000]{1,0:T(8,128)(2,1)} async-done(((bf16[32,1000]{1,0:T(8,128)(2,1)}), bf16[1024,1000]{1,0:T(8,128)(2,1)}) %all-gather.30.cloned.1.call-update) | async-done | bytes 2048016 | tf_op jit(solution)/shard_map/all_gather | solution.py:382
  795.4 5.6 convolution_convert_fusion.12
  851.4 8.0 fusion.32
  914.5 39.6 %all-reduce.1 = (f32[]{:T(128)}, f32[]{:T(128)}, f32[6381]{0:T(1024)}) all-reduce(f32[]{:T(128)S(6)} %mul.684, f32[]{:T(128)} %bitcast, f32[6381]{0:T(1024)S(1)} %concatenate.8), channel_id=1, replica_groups=mesh['dp'=8,'head'=4] {'dp','head'}, use_global_device_ids=true, to_apply=%region_21.22 | all-reduce | flops 6383 | bytes 51064 | tf_op jit(solution)/shard_map/psum | solution.py:422
  954.1 40.7 %all-gather.10 = bf16[32768]{0:T(1024)(128)(2,1)S(1)} all-gather(bf16[1024]{0:T(1024)(128)(2,1)S(1)} %multiply_convert_fusion.12), channel_id=12, replica_groups=mesh['dp'=8,'head'=4] {'dp','head'}, dimensions={0}, use_global_device_ids=true | all-gather | bytes 67584 | tf_op jit(solution)/shard_map/all_gather | solution.py:424
  1000.6 60.9 %reduce-scatter.35.cloned.1.call-done = bf16[64,261]{1,0:T(8,128)(2,1)} async-done(((bf16[2048,261]{1,0:T(8,128)(2,1)}), bf16[64,261]{1,0:T(8,128)(2,1)}) %reduce-scatter.35.cloned.1.call-update) | async-done | bytes 33424 | tf_op jit(solution)/shard_map/reduce_scatter | solution.py:386
  1063.0 134.3 %reduce-scatter.37.cloned.1.call-done = bf16[32,512]{1,0:T(8,128)(2,1)} async-done(((bf16[1024,512]{1,0:T(8,128)(2,1)}), bf16[32,512]{1,0:T(8,128)(2,1)}) %reduce-scatter.37.cloned.1.call-update) | async-done | bytes 32784 | tf_op jit(solution)/shard_map/reduce_scatter | solution.py:386
  1199.0 132.9 %reduce-scatter.15.cloned.1.call-done = bf16[32,1024]{1,0:T(8,128)(2,1)} async-done(((bf16[1024,1024]{1,0:T(8,128)(2,1)}), bf16[32,1024]{1,0:T(8,128)(2,1)}) %reduce-scatter.15.cloned.1.call-update) | async-done | bytes 65552 | tf_op jit(solution)/shard_map/reduce_scatter | solution.py:386
  1332.7 133.6 %reduce-scatter.17.cloned.1.call-done = bf16[32,1024]{1,0:T(8,128)(2,1)} async-done(((bf16[1024,1024]{1,0:T(8,128)(2,1)}), bf16[32,1024]{1,0:T(8,128)(2,1)}) %reduce-scatter.17.cloned.1.call-update) | async-done | bytes 65552 | tf_op jit(solution)/shard_map/reduce_scatter | solution.py:386
  1467.1 133.8 %reduce-scatter.19.cloned.1.call-done = bf16[32,1024]{1,0:T(8,128)(2,1)} async-done(((bf16[1024,1024]{1,0:T(8,128)(2,1)}), bf16[32,1024]{1,0:T(8,128)(2,1)}) %reduce-scatter.19.cloned.1.call-update) | async-done | bytes 65552 | tf_op jit(solution)/shard_map/reduce_scatter | solution.py:386
  1601.8 134.0 %reduce-scatter.21.cloned.1.call-done = bf16[32,1024]{1,0:T(8,128)(2,1)} async-done(((bf16[1024,1024]{1,0:T(8,128)(2,1)}), bf16[32,1024]{1,0:T(8,128)(2,1)}) %reduce-scatter.21.cloned.1.call-update) | async-done | bytes 65552 | tf_op jit(solution)/shard_map/reduce_scatter | solution.py:386
  1736.6 134.0 %reduce-scatter.23.cloned.1.call-done = bf16[32,1024]{1,0:T(8,128)(2,1)} async-done(((bf16[1024,1024]{1,0:T(8,128)(2,1)}), bf16[32,1024]{1,0:T(8,128)(2,1)}) %reduce-scatter.23.cloned.1.call-update) | async-done | bytes 65552 | tf_op jit(solution)/shard_map/reduce_scatter | solution.py:386
  1871.5 134.1 %reduce-scatter.25.cloned.1.call-done = bf16[32,1024]{1,0:T(8,128)(2,1)} async-done(((bf16[1024,1024]{1,0:T(8,128)(2,1)}), bf16[32,1024]{1,0:T(8,128)(2,1)}) %reduce-scatter.25.cloned.1.call-update) | async-done | bytes 65552 | tf_op jit(solution)/shard_map/reduce_scatter | solution.py:386
  2006.4 134.0 %reduce-scatter.27.cloned.1.call-done = bf16[32,1024]{1,0:T(8,128)(2,1)} async-done(((bf16[1024,1024]{1,0:T(8,128)(2,1)}), bf16[32,1024]{1,0:T(8,128)(2,1)}) %reduce-scatter.27.cloned.1.call-update) | async-done | bytes 65552 | tf_op jit(solution)/shard_map/reduce_scatter | solution.py:386
  2141.3 133.9 %reduce-scatter.29.cloned.1.call-done = bf16[32,1024]{1,0:T(8,128)(2,1)} async-done(((bf16[1024,1024]{1,0:T(8,128)(2,1)}), bf16[32,1024]{1,0:T(8,128)(2,1)}) %reduce-scatter.29.cloned.1.call-update) | async-done | bytes 65552 | tf_op jit(solution)/shard_map/reduce_scatter | solution.py:386
  2276.0 134.0 %reduce-scatter.31.cloned.1.call-done = bf16[32,1024]{1,0:T(8,128)(2,1)} async-done(((bf16[1024,1024]{1,0:T(8,128)(2,1)}), bf16[32,1024]{1,0:T(8,128)(2,1)}) %reduce-scatter.31.cloned.1.call-update) | async-done | bytes 65552 | tf_op jit(solution)/shard_map/reduce_scatter | solution.py:386
  2410.9 133.9 %reduce-scatter.33.cloned.1.call-done = bf16[32,1024]{1,0:T(8,128)(2,1)} async-done(((bf16[1024,1024]{1,0:T(8,128)(2,1)}), bf16[32,1024]{1,0:T(8,128)(2,1)}) %reduce-scatter.33.cloned.1.call-update) | async-done | bytes 65552 | tf_op jit(solution)/shard_map/reduce_scatter | solution.py:386
  (359 shorter events, 231.5 us)
Async XLA Ops:
  7.2 60.7 %all-gather.26.cloned.1.call-start = ((), (), s32[]{:S(2)}) async-start(), calls=%async_computation.13 | async-start | bytes 1081344 | tf_op jit(solution)/shard_map/all_gather | solution.py:382
  8.8 116.5 %all-gather.28.cloned.1.call-start = ((), (), s32[]{:S(2)}) async-start(), calls=%async_computation.14 | async-start | bytes 1622016 | tf_op jit(solution)/shard_map/all_gather | solution.py:382
  10.4 173.6 %all-gather.32.cloned.1.call-start = ((), (), s32[]{:S(2)}) async-start(), calls=%async_computation.27 | async-start | bytes 2162688 | tf_op jit(solution)/shard_map/all_gather | solution.py:382
  12.8 229.7 %all-gather.34.cloned.1.call-start = ((), (), s32[]{:S(2)}) async-start(), calls=%async_computation.28 | async-start | bytes 2162688 | tf_op jit(solution)/shard_map/all_gather | solution.py:382
  13.3 287.7 %all-gather.36.cloned.1.call-start = ((), (), s32[]{:S(2)}) async-start(), calls=%async_computation.29 | async-start | bytes 2162688 | tf_op jit(solution)/shard_map/all_gather | solution.py:382
  13.9 345.7 %all-gather.38.cloned.1.call-start = ((), (), s32[]{:S(2)}) async-start(), calls=%async_computation.30 | async-start | bytes 2162688 | tf_op jit(solution)/shard_map/all_gather | solution.py:382
  14.5 403.8 %all-gather.44.cloned.1.call-start = ((), (), s32[]{:S(2)}) async-start(), calls=%async_computation.33 | async-start | bytes 2162688 | tf_op jit(solution)/shard_map/all_gather | solution.py:382
  15.3 461.7 %all-gather.42.cloned.1.call-start = ((), (), s32[]{:S(2)}) async-start(), calls=%async_computation.32 | async-start | bytes 2162688 | tf_op jit(solution)/shard_map/all_gather | solution.py:382
  16.0 519.7 %all-gather.40.cloned.1.call-start = ((), (), s32[]{:S(2)}) async-start(), calls=%async_computation.31 | async-start | bytes 2162688 | tf_op jit(solution)/shard_map/all_gather | solution.py:382
  16.7 577.5 %all-gather.46.cloned.1.call-start = ((), (), s32[]{:S(2)}) async-start(), calls=%async_computation.34 | async-start | bytes 2162688 | tf_op jit(solution)/shard_map/all_gather | solution.py:382
  17.3 635.6 %all-gather.48.cloned.1.call-start = ((), (), s32[]{:S(2)}) async-start(), calls=%async_computation.35 | async-start | bytes 2162688 | tf_op jit(solution)/shard_map/all_gather | solution.py:382
  18.1 693.4 %all-gather.50.cloned.1.call-start = ((), (), s32[]{:S(2)}) async-start(), calls=%async_computation.36 | async-start | bytes 2162688 | tf_op jit(solution)/shard_map/all_gather | solution.py:382
  19.4 10.3 all-to-all-start
  23.6 746.5 %all-gather.30.cloned.1.call-start = ((), (), s32[]{:S(2)}) async-start(), calls=%async_computation.15 | async-start | bytes 2162688 | tf_op jit(solution)/shard_map/all_gather | solution.py:382
  24.3 973.3 %all-reduce.4.cloned.1.call-start = ((), (), s32[]{:S(2)}) async-start(), calls=%async_computation.37 | async-start | bytes 262144
  29.8 809.1 %copy-start.64 = (f32[512]{0:T(512)}, f32[512]{0:T(512)S(1)}, u32[]{:S(2)}) copy-start(f32[512]{0:T(512)S(1)} %get-tuple-element.137) | copy-start | bytes 6148
  29.9 809.0 %copy-start.66 = (f32[512]{0:T(512)}, f32[512]{0:T(512)S(1)}, u32[]{:S(2)}) copy-start(f32[512]{0:T(512)S(1)} %rsqrt_bitcast_fusion) | copy-start | bytes 6148
  838.9 222.6 %reduce-scatter.35.cloned.1.call-start = ((), (), s32[]{:S(2)}) async-start(), calls=%async_computation.26 | async-start | bytes 1622016 | tf_op jit(solution)/shard_map/reduce_scatter | solution.py:386
  848.0 349.4 %reduce-scatter.37.cloned.1.call-start = ((), (), s32[]{:S(2)}) async-start(), calls=%async_computation.38 | async-start | bytes 1081344 | tf_op jit(solution)/shard_map/reduce_scatter | solution.py:386
  861.7 470.1 %reduce-scatter.15.cloned.1.call-start = ((), (), s32[]{:S(2)}) async-start(), calls=%async_computation.16 | async-start | bytes 2162688 | tf_op jit(solution)/shard_map/reduce_scatter | solution.py:386
  865.9 600.3 %reduce-scatter.17.cloned.1.call-start = ((), (), s32[]{:S(2)}) async-start(), calls=%async_computation.17 | async-start | bytes 2162688 | tf_op jit(solution)/shard_map/reduce_scatter | solution.py:386
  871.0 729.9 %reduce-scatter.19.cloned.1.call-start = ((), (), s32[]{:S(2)}) async-start(), calls=%async_computation.18 | async-start | bytes 2162688 | tf_op jit(solution)/shard_map/reduce_scatter | solution.py:386
  875.1 860.7 %reduce-scatter.21.cloned.1.call-start = ((), (), s32[]{:S(2)}) async-start(), calls=%async_computation.19 | async-start | bytes 2162688 | tf_op jit(solution)/shard_map/reduce_scatter | solution.py:386
  881.2 989.5 %reduce-scatter.23.cloned.1.call-start = ((), (), s32[]{:S(2)}) async-start(), calls=%async_computation.20 | async-start | bytes 2162688 | tf_op jit(solution)/shard_map/reduce_scatter | solution.py:386
  885.3 1120.2 %reduce-scatter.25.cloned.1.call-start = ((), (), s32[]{:S(2)}) async-start(), calls=%async_computation.21 | async-start | bytes 2162688 | tf_op jit(solution)/shard_map/reduce_scatter | solution.py:386
  889.2 1251.2 %reduce-scatter.27.cloned.1.call-start = ((), (), s32[]{:S(2)}) async-start(), calls=%async_computation.22 | async-start | bytes 2162688 | tf_op jit(solution)/shard_map/reduce_scatter | solution.py:386
  893.1 1382.1 %reduce-scatter.29.cloned.1.call-start = ((), (), s32[]{:S(2)}) async-start(), calls=%async_computation.23 | async-start | bytes 2162688 | tf_op jit(solution)/shard_map/reduce_scatter | solution.py:386
  897.3 1512.8 %reduce-scatter.31.cloned.1.call-start = ((), (), s32[]{:S(2)}) async-start(), calls=%async_computation.24 | async-start | bytes 2162688 | tf_op jit(solution)/shard_map/reduce_scatter | solution.py:386
  903.0 1641.9 %reduce-scatter.33.cloned.1.call-start = ((), (), s32[]{:S(2)}) async-start(), calls=%async_computation.25 | async-start | bytes 2162688 | tf_op jit(solution)/shard_map/reduce_scatter | solution.py:386
  914.4 283.0 %copy-start.53 = (f32[512,32]{0,1:T(8,128)S(1)}, f32[512,32]{0,1:T(8,128)}, u32[]{:S(2)}) copy-start(f32[512,32]{0,1:T(8,128)} %param.26) | copy-start | bytes 196612
  994.8 1550.9 %copy-start.24 = (f32[10,32,1024]{2,1,0:T(8,128)S(1)}, f32[10,32,1024]{2,1,0:T(8,128)}, u32[]{:S(2)}) copy-start(f32[10,32,1024]{2,1,0:T(8,128)} %param.23) | copy-start | bytes 3932164
  994.8 1550.9 %copy-start.38 = (f32[10,32,1024]{2,1,0:T(8,128)S(1)}, f32[10,32,1024]{2,1,0:T(8,128)}, u32[]{:S(2)}) copy-start(f32[10,32,1024]{2,1,0:T(8,128)} %param.33) | copy-start | bytes 3932164
  (78 other events, 1266.2 us)
Sparse Core Ops, SparseCore 0:
  11.5 56.3 all-gather.25
  71.3 53.8 all-gather.27
  128.7 55.2 all-gather.31
  187.3 55.2 all-gather.33
  245.8 55.2 all-gather.35
  304.3 55.2 all-gather.37
  363.0 55.2 all-gather.43
  421.7 55.2 all-gather.41
  480.4 55.2 all-gather.39
  539.0 55.2 all-gather.45
  597.6 55.2 all-gather.47
  656.2 55.2 all-gather.49
  714.9 55.2 all-gather.29
  839.0 121.2 all-reduce.3
  965.4 96.0 reduce-scatter.34
  1063.6 133.7 reduce-scatter.36
  1199.6 132.2 reduce-scatter.14
  1334.0 132.2 reduce-scatter.16
  1468.6 132.2 reduce-scatter.18
  1603.0 132.6 reduce-scatter.20
  1738.1 132.4 reduce-scatter.22
  1872.9 132.6 reduce-scatter.24
  2007.9 132.4 reduce-scatter.26
  2142.5 132.6 reduce-scatter.28
  2277.5 132.4 reduce-scatter.30
  2412.2 132.6 reduce-scatter.32

commit v2 on v1

--- a/solution.py
+++ b/solution.py
@@ -1,8 +1,11 @@
+import functools
 import math
 
 import jax
 import jax.numpy as jnp
 from jax import lax
+from jax.experimental import pallas as pl
+from jax.experimental.pallas import tpu as pltpu
 from jax.sharding import PartitionSpec as P
 
 D = 1024
@@ -300,6 +303,284 @@
     return tuple(results)
 
 
+MESH=pl.DeviceIdType.MESH
+MB=1<<20
+GAP=2
+
+def where_am_i():
+    dp=lax.axis_index("dp"); h=lax.axis_index("head")
+    return dict(dp=dp,h=h,z=dp//2,y=dp%2,x=h//2,c=h%2)
+
+def neighbours(me):
+    return dict(zu=(me["dp"]+2,me["h"]),zd=(me["dp"]-2,me["h"]),y=(me["dp"]+1-2*me["y"],me["h"]),
+                x=(me["dp"],me["h"]+2-4*me["x"]),c=(me["dp"],me["h"]+1-2*me["c"]))
+
+def entry_barrier(me,nb,others=()):
+    z=me["z"]
+    bar=pltpu.get_barrier_semaphore()
+    for k in ("x","y","c"):
+        pl.semaphore_signal(bar,inc=1,device_id=nb[k],device_id_type=MESH)
+    @pl.when(z<3)
+    def _(): pl.semaphore_signal(bar,inc=1,device_id=nb["zu"],device_id_type=MESH)
+    @pl.when(z>0)
+    def _(): pl.semaphore_signal(bar,inc=1,device_id=nb["zd"],device_id_type=MESH)
+    for other in others:
+        pl.semaphore_signal(bar,inc=1,device_id=other,device_id_type=MESH)
+    pl.semaphore_wait(bar,4+(z+1)//2%2+len(others))
+
+class Gather:
+    def __init__(self,me,nb,buf,groups,ssem,rsem):
+        self.me,self.nb,self.buf,self.groups,self.ssem,self.rsem=me,nb,buf,groups,ssem,rsem
+        self.pending=[]
+    def copy(self,src,dst,slot,dev):
+        return pltpu.make_async_remote_copy(src_ref=src,dst_ref=dst,send_sem=self.ssem.at[slot],recv_sem=self.rsem.at[slot],device_id=dev,device_id_type=MESH)
+    def view(self,r,*ix):
+        return self.buf.at[(*ix,slice(None),pl.ds(*self.groups[r]))]
+    def hop(self,r,k,op):
+        z,y,x,c=(self.me[i] for i in "zyxc")
+        rest=(y,x,c) if r<2 else (slice(None),slice(None),c)
+        su,sd=8*r+k-1,8*r+3+k-1
+        if op=="start":
+            @pl.when((z<3)&(z>=k-1))
+            def _():
+                v=self.view(r,z-(k-1),*rest); self.copy(v,v,su,self.nb["zu"]).start()
+            @pl.when((z>0)&(z+k-1<=3))
+            def _():
+                v=self.view(r,z+(k-1),*rest); self.copy(v,v,sd,self.nb["zd"]).start()
+        elif op=="recv":
+            @pl.when(z>=k)
+            def _():
+                v=self.view(r,z-k,*rest); self.copy(v,v,su,self.nb["zd"]).wait_recv()
+            @pl.when(z+k<=3)
+            def _():
+                v=self.view(r,z+k,*rest); self.copy(v,v,sd,self.nb["zu"]).wait_recv()
+        else:
+            @pl.when((z<3)&(z>=k-1))
+            def _():
+                v=self.view(r,z-(k-1),*rest); self.copy(v,v,su,self.nb["zu"]).wait_send()
+            @pl.when((z>0)&(z+k-1<=3))
+            def _():
+                v=self.view(r,z+(k-1),*rest); self.copy(v,v,sd,self.nb["zd"]).wait_send()
+    def flat(self,r,axis,op):
+        z,y,x,c=(self.me[i] for i in "zyxc")
+        A=slice(None)
+        if axis=="y":
+            mine={0:(A,y,x,c),1:(A,y,A,c),2:(z,y,A,c)}[r]; other={0:(A,1-y,x,c),1:(A,1-y,A,c),2:(z,1-y,A,c)}[r]; slot=8*r+6
+        elif axis=="x":
+            mine={0:(A,A,x,c),1:(A,y,x,c),2:(z,y,x,c)}[r]; other={0:(A,A,1-x,c),1:(A,y,1-x,c),2:(z,y,1-x,c)}[r]; slot=8*r+7
+        if op=="start":
+            v=self.view(r,*mine); self.copy(v,v,slot,self.nb[axis]).start()
+        elif op=="recv":
+            v=self.view(r,*other); self.copy(v,v,slot,self.nb[axis]).wait_recv()
+        else:
+            v=self.view(r,*mine); self.copy(v,v,slot,self.nb[axis]).wait_send()
+    def core(self,op):
+        c=self.me["c"]; A=slice(None)
+        if op=="recv":
+            v=self.buf.at[A,A,A,1-c]; self.copy(v,v,24,self.nb["c"]).wait_recv()
+        else:
+            v=self.buf.at[A,A,A,c]; d=self.copy(v,v,24,self.nb["c"])
+            d.start() if op=="start" else d.wait_send()
+    ORDER=[["h1","h2","h3","y","x"],["h1","h2","h3","x","y"],["x","y","h1","h2","h3"]]
+    def do(self,r,p,op):
+        n=self.ORDER[r][p]
+        if n[0]=="h": self.hop(r,int(n[1]),op)
+        else: self.flat(r,n,op)
+    NPH=6
+    def phase(self,p):
+        if p>0 and p<=5:
+            for r in range(3):
+                if self.groups[r][1]: self.do(r,p-1,"recv")
+                if p<5 and self.groups[r][1]: self.do(r,p,"start")
+        if p==0:
+            for r in range(3):
+                if self.groups[r][1]: self.do(r,0,"start")
+        if p==5: self.core("start")
+        if p==6: self.core("recv")
+    def sends(self):
+        for r in range(3):
+            if self.groups[r][1]:
+                for p in range(5): self.do(r,p,"send")
+        self.core("send")
+
+SPLIT={1024:((0,384),(384,384),(768,256)),512:((0,128),(128,256),(384,128)),384:((0,128),(128,128),(256,128))}
+
+def gather_kernel(nt,*refs):
+    shards=refs[:nt]; bufs=refs[nt:2*nt]; lsem,ssem,rsem=refs[2*nt:]
+    me=where_am_i(); nb=neighbours(me)
+    z,y,x,c=(me[i] for i in "zyxc")
+    local=[pltpu.make_async_copy(s,b.at[z,y,x,c],lsem.at[i]) for i,(s,b) in enumerate(zip(shards,bufs))]
+    for l in local: l.start()
+    entry_barrier(me,nb)
+    gs=[Gather(me,nb,b,SPLIT[b.shape[-1]],ssem.at[i],rsem.at[i]) for i,b in enumerate(bufs)]
+    for tick in range(nt+6*GAP):
+        for t in range(nt):
+            p=tick-t
+            if p==0: local[t].wait()
+            if p>=0 and p%GAP==0 and p//GAP<=6: gs[t].phase(p//GAP)
+    for g in gs: g.sends()
+
+def gather_all(shards,cid=0):
+    nt=len(shards)
+    outs=[jax.ShapeDtypeStruct((4,2,2,2)+s.shape,s.dtype) for s in shards]
+    return pl.pallas_call(functools.partial(gather_kernel,nt),out_shape=outs,
+        in_specs=[pl.BlockSpec(memory_space=pl.ANY)]*nt,out_specs=[pl.BlockSpec(memory_space=pl.ANY)]*nt,
+        scratch_shapes=[pltpu.SemaphoreType.DMA((nt,)),pltpu.SemaphoreType.DMA((nt,25)),pltpu.SemaphoreType.DMA((nt,25))],
+        compiler_params=pltpu.CompilerParams(collective_id=cid,has_side_effects=True,vmem_limit_bytes=60*MB))(*shards)
+
+
+ALLS=slice(None)
+
+def recv_shapes(r,n):
+    (_,a),(_,b),(_,c)=SPLIT[n]
+    return dict(core=(4,2,2,r,n),A0=(4,2,r,a),A1=(4,r,a),Ah=(6,r,a),B0=(4,2,r,b),B1=(4,r,b),Bh=(6,r,b),Ch=(6,2,2,r,c),C0=(2,r,c),C1=(r,c))
+RNAMES=("core","A0","A1","Ah","B0","B1","Bh","Ch","C0","C1")
+
+def add_into(dst,src,cols,lead):
+    for di,si in lead:
+        dst[(*di,ALLS,cols)]=dst[(*di,ALLS,cols)]+src[si]
+
+class Scatter:
+    def __init__(self,me,nb,part,send_half,bufs,out,groups,ssem,rsem):
+        self.me,self.nb,self.part,self.half,self.b,self.out,self.groups,self.ssem,self.rsem=me,nb,part,send_half,bufs,out,groups,ssem,rsem
+    def copy(self,src,dst,slot,dev):
+        return pltpu.make_async_remote_copy(src_ref=src,dst_ref=dst,send_sem=self.ssem.at[slot],recv_sem=self.rsem.at[slot],device_id=dev,device_id_type=MESH)
+    def cols(self,r): return pl.ds(*self.groups[r])
+    def hop(self,r,k,op):
+        z,y,x=(self.me[i] for i in "zyx")
+        rest=(y,x) if r<2 else (ALLS,ALLS)
+        buf=self.b["ABC"[r]+"h"]; cols=self.cols(r)
+        su,sd=8*r+k-1,8*r+3+k-1
+        up=lambda: self.copy(self.part.at[(z+k,*rest,ALLS,cols)],buf.at[k-1],su,self.nb["zu"])
+        dn=lambda: self.copy(self.part.at[(z-k,*rest,ALLS,cols)],buf.at[3+k-1],sd,self.nb["zd"])
+        if op in("start","send"):
+            @pl.when(z+k<=3)
+            def _():
+                d=up(); d.start() if op=="start" else d.wait_send()
+            @pl.when(z-k>=0)
+            def _():
+                d=dn(); d.start() if op=="start" else d.wait_send()
+        else:
+            last=(k==1 and r<2)
+            @pl.when((z>=1)&(z-1+k<=3))
+            def _():
+                self.copy(buf.at[k-1],buf.at[k-1],su,self.nb["zd"]).wait_recv()
+                self.hopadd(r,z-1+k,buf.at[k-1],cols)
+            @pl.when((z<=2)&(z+1-k>=0))
+            def _():
+                self.copy(buf.at[3+k-1],buf.at[3+k-1],sd,self.nb["zu"]).wait_recv()
+                self.hopadd(r,z+1-k,buf.at[3+k-1],cols)
+    def hopadd(self,r,d,src,cols):
+        y,x=self.me["y"],self.me["x"]
+        if r<2: add_into(self.part,src,cols,[((d,y,x),(ALLS,ALLS))])
+        else: add_into(self.part,src,cols,[((d,i,j),(i,j)) for i in range(2) for j in range(2)])
+    def flat(self,r,axis,op):
+        z,y,x=(self.me[i] for i in "zyx"); cols=self.cols(r)
+        name="ABC"[r]
+        if axis=="x":
+            mine={0:(ALLS,ALLS,1-x),1:(ALLS,y,1-x),2:(z,y,1-x)}[r]; slot=8*r+7; buf=self.b[{0:"A0",1:"B1",2:"C1"}[r]]
+        else:
+            mine={0:(ALLS,1-y,x),1:(ALLS,1-y),2:(z,1-y)}[r]; slot=8*r+6; buf=self.b[{0:"A1",1:"B0",2:"C0"}[r]]
+        if op=="recv":
+            self.copy(buf,buf,slot,self.nb[axis]).wait_recv()
+            if axis=="x":
+                lead={0:[((i,j,x),(i,j)) for i in range(4) for j in range(2)],1:[((i,y,x),(i,)) for i in range(4)],2:[((z,y,x),(ALLS,ALLS))]}[r]
+            else:
+                lead={0:[((i,y,x),(i,)) for i in range(4)],1:[((i,y,j),(i,j)) for i in range(4) for j in range(2)],2:[((z,y,j),(j,)) for j in range(2)]}[r]
+            add_into(self.part,buf,cols,lead)
+        else:
+            d=self.copy(self.part.at[(*mine,)+(ALLS,)*(4-len(mine))+(cols,)],buf,slot,self.nb[axis])
+            d.start() if op=="start" else d.wait_send()
+    def core(self,op):
+        buf=self.b["core"]
+        if op=="recv":
+            self.copy(buf,buf,24,self.nb["c"]).wait_recv()
+            @pl.loop(0,4)
+            def _(i):
+                for j in range(2):
+                    for k in range(2):
+                        self.part[i,j,k]=self.part[i,j,k]+buf[i,j,k]
+        else:
+            d=self.copy(self.half,buf,24,self.nb["c"]); d.start() if op=="start" else d.wait_send()
+    ORDER=[["x","y","h3","h2","h1"],["y","x","h3","h2","h1"],["h3","h2","h1","y","x"]]
+    def do(self,r,p,op):
+        n=self.ORDER[r][p]
+        if n[0]=="h": self.hop(r,int(n[1]),op)
+        else: self.flat(r,n,op)
+    def phase(self,p):
+        if p==0: self.core("start"); return
+        if p==1: self.core("recv")
+        for r in range(3):
+            if p>=2: self.do(r,p-2,"recv")
+            if p<=5: self.do(r,p-1,"start")
+        if p==6:
+            z,y,x=(self.me[i] for i in "zyx")
+            self.out[...]=self.part[z,y,x].astype(jnp.float32)
+    def sends(self):
+        self.core("send")
+        for r in range(3):
+            for p in range(5): self.do(r,p,"send")
+
+def small_steps(me):
+    dp,h=me["dp"],me["h"]
+    z=me["z"]
+    return [(dp,h+1-2*me["c"]),(dp,h+2-4*me["x"]),(dp+1-2*me["y"],h),(dp+2-4*(z%2),h),(dp+4-8*(z//2),h)]
+
+def scatter_kernel(nt,gap,*refs):
+    parts_in=refs[:nt]; vec,small=refs[nt:nt+2]
+    outs=refs[nt+2:2*nt+2]; vec_out,small_out=refs[2*nt+2:2*nt+4]
+    rest=list(refs[2*nt+4:])
+    part=[rest.pop(0) for _ in range(nt)]
+    bufs=[{k:rest.pop(0) for k in RNAMES} for _ in range(nt)]
+    vbuf,srecv,ssend,lsem,ssem,rsem,vs,vr,sms,smr=rest
+    me=where_am_i(); nb=neighbours(me)
+    z,y,x,c=(me[i] for i in "zyxc")
+    local=[pltpu.make_async_copy(d.at[:,:,:,c],p,lsem.at[i]) for i,(d,p) in enumerate(zip(parts_in,part))]
+    for l in local: l.start()
+    vbuf[z,y,x,c]=vec[...]
+    entry_barrier(me,nb,small_steps(me)[4:])
+    gs=[Scatter(me,nb,part[i],parts_in[i].at[:,:,:,1-c],bufs[i],outs[i],SPLIT[part[i].shape[-1]],ssem.at[i],rsem.at[i]) for i in range(nt)]
+    gv=Gather(me,nb,vbuf,[(0,0),(0,0),(0,vbuf.shape[-1])],vs,vr)
+    acc=small[...]
+    sm=[]
+    for i,p in enumerate(small_steps(me)):
+        sm.append(pltpu.make_async_remote_copy(src_ref=ssend.at[i],dst_ref=srecv.at[i],send_sem=sms.at[i],recv_sem=smr.at[i],device_id=p,device_id_type=MESH))
+    ssend[0]=small[...]
+    for tick in range(nt+6*gap):
+        if tick%2==0 and tick//2<=5:
+            i=tick//2
+            if i>0:
+                sm[i-1].wait_recv()
+                s=ssend[i-1]+srecv[i-1]
+                if i<5: ssend[i]=s
+                else: small_out[...]=s
+            if i<5: sm[i].start()
+        if tick%gap==0 and tick//gap<=6: gv.phase(tick//gap)
+        for t in range(nt):
+            p=tick-t
+            if p==0: local[t].wait()
+            if p>=0 and p%gap==0 and p//gap<=6: gs[t].phase(p//gap)
+    for s in sm: s.wait_send()
+    gv.sends()
+    vec_out[...]=vbuf[...]
+    for g in gs: g.sends()
+
+def scatter_all(parts,vec,small,cid=1,gap=2):
+    nt=len(parts)
+    outs=[jax.ShapeDtypeStruct(p.shape[-2:],jnp.float32) for p in parts]+[jax.ShapeDtypeStruct((4,2,2,2)+vec.shape,vec.dtype),jax.ShapeDtypeStruct(small.shape,small.dtype)]
+    V=pl.BlockSpec(memory_space=pltpu.VMEM)
+    D=pltpu.SemaphoreType.DMA
+    scr=[pltpu.VMEM((4,2,2)+p.shape[-2:],jnp.bfloat16) for p in parts]
+    for p in parts:
+        sh=recv_shapes(*p.shape[-2:])
+        scr+=[pltpu.VMEM(sh[k],jnp.bfloat16) for k in RNAMES]
+    scr+=[pltpu.VMEM((4,2,2,2)+vec.shape,vec.dtype),pltpu.VMEM((5,)+small.shape,small.dtype),pltpu.VMEM((5,)+small.shape,small.dtype),
+          D((nt,)),D((nt,25)),D((nt,25)),D((25,)),D((25,)),D((5,)),D((5,))]
+    return pl.pallas_call(functools.partial(scatter_kernel,nt,gap),out_shape=outs,
+        in_specs=[pl.BlockSpec(memory_space=pl.ANY)]*nt+[V,V],out_specs=[V]*(nt+2),scratch_shapes=scr,
+        compiler_params=pltpu.CompilerParams(collective_id=cid,has_side_effects=True,vmem_limit_bytes=62*MB))(*parts,vec,small)
+
+
 def image_forward_back(weights, small, pixels, mask_row, valid_one, label):
     square, kv_weight, head_weight, latent_all = weights
     gains = small[: 5 * D].reshape(5, D)
@@ -310,7 +591,8 @@
     valid_keys = mask_row > 0
     pix_float = pixels.astype(jnp.float32)
     normed_pix = layer_norm(pix_float, pix_gain).astype(jnp.bfloat16)
-    kv = dot_nn(normed_pix, kv_weight).astype(jnp.bfloat16)
+    normed_pix = jnp.pad(normed_pix, ((0, 0), (0, kv_weight.shape[1] - CIN)))
+    kv = dot_nt(normed_pix, kv_weight).astype(jnp.bfloat16)
     keys_px = kv[:, :D].reshape(-1, 1, D)
     values_px = kv[:, D:].reshape(-1, 1, D)
     query_norm = layer_norm(latent, gains[0]).astype(jnp.bfloat16)
@@ -327,7 +609,7 @@
     hidden4, mlp_second = mlp_forward(hidden3, gains[3], square[8], square[9])
     final = layer_norm(hidden4, gains[4])
     pooled_b = (jnp.sum(final, axis=0) / rows).astype(jnp.bfloat16)
-    logits = dot_nn(pooled_b[None, :], head_weight)[0] + bias
+    logits = dot_nn(pooled_b[None, :], head_weight)[0, : bias.shape[0]] + bias
     logp = jax.nn.log_softmax(logits)
     picked = jnp.arange(logits.shape[0]) == label
     loss = -valid_one * (
@@ -335,7 +617,7 @@
     )
     target = (1.0 - SMOOTH) * picked.astype(jnp.float32) + SMOOTH / logits.shape[0]
     d_logits = valid_one * (jnp.exp(logp) - target)
-    d_pooled = jnp.dot(head_weight.astype(jnp.float32), d_logits)
+    d_pooled = jnp.dot(head_weight[:, : bias.shape[0]].astype(jnp.float32), d_logits)
     d_final = jnp.broadcast_to(d_pooled / rows, final.shape)
     d_hidden4, d_gain4 = jax.vjp(layer_norm, hidden4, gains[4])[1](d_final)
     d_hidden3, d_gain3, d_w8, d_w9 = mlp_backward(
@@ -361,7 +643,7 @@
     )
     d_kv_px = jnp.concatenate([d_keys.reshape(-1, D), d_values.reshape(-1, D)], axis=1).astype(jnp.bfloat16)
     d_kv_turned = dot_tn(d_kv_px, normed_pix)
-    d_normed_pix = dot_nt(d_kv_px, kv_weight)
+    d_normed_pix = dot_nn(d_kv_px, kv_weight)[:, :CIN]
     d_pix_gain = jax.vjp(layer_norm, pix_float, pix_gain)[1](d_normed_pix)[1]
     d_query_b = d_query.reshape(rows, D).astype(jnp.bfloat16)
     d_w0 = dot_tn(query_norm, d_query_b)
@@ -373,17 +655,6 @@
         [d_gain0, d_gain1, d_gain2, d_gain3, d_gain4, d_pix_gain, d_logits]
     )
     return d_square, d_kv_turned, d_latent.T, d_small, pooled_b, d_logits, loss
-
-
-ALL = ("dp", "head")
-
-
-def gather_rows(shard):
-    return lax.all_gather(shard, ALL, axis=0, tiled=True)
-
-
-def scatter_rows(partial):
-    return lax.psum_scatter(partial.astype(jnp.bfloat16), ALL, scatter_dimension=0, tiled=True).astype(jnp.float32)
 
 
 def per_device_images(
@@ -411,26 +682,32 @@
     micro = lax.axis_index("head")
     pick = lambda a: lax.dynamic_index_in_dim(a, micro, 0, keepdims=False)[0]
     image = lax.all_to_all(pixels[:, 0], "head", split_axis=0, concat_axis=1, tiled=True)[0]
-    latent_all = gather_rows(latents.astype(bf).T).T
-    kv_all = gather_rows(kv_weight.astype(bf).T).T
-    square_all = [gather_rows(square[i].astype(bf)) for i in range(10)]
-    head_all = gather_rows(head_weight.astype(bf))
-    valid_float = valid.astype(jnp.float32)
+    classes = head_weight.shape[1]
+    shards = [latents.astype(bf).T, jnp.pad(kv_weight.astype(bf).T, ((0, 0), (0, 384 - CIN)))]
+    shards += [square[i].astype(bf) for i in range(10)]
+    shards += [jnp.pad(head_weight.astype(bf), ((0, 0), (0, D - classes)))]
+    whole = [w.reshape(-1, w.shape[-1]) for w in gather_all(shards)]
     d_square, d_kv, d_lat, d_small, pooled_b, d_logits, loss = image_forward_back(
-        (square_all, kv_all, head_all, latent_all), small, image, pick(masks), pick(valid_float), pick(labels)
-    )
-    small_total, loss_sum, count = lax.psum((d_small, loss, pick(valid_float)), ALL)
+        (whole[2:12], whole[1], whole[12], whole[0].T), small, image,
+        pick(masks), pick(valid.astype(jnp.float32)), pick(labels),
+    )
+    parts = [d.astype(bf).reshape((4, 2, 2, 2, -1, d.shape[-1])) for d in d_square + [d_kv, d_lat]]
+    pad = lambda v, n: jnp.pad(v, (0, n - v.shape[0]))
+    vec = jnp.concatenate([pooled_b.astype(jnp.float32), pad(d_logits, D)]).reshape(8, 256)
+    counted = jnp.stack([loss, pick(valid.astype(jnp.float32))])
+    packed = pad(jnp.concatenate([d_small, counted]), 56 * 128).reshape(56, 128)
+    *own, vec_all, packed = scatter_all(parts, vec, packed)
+    packed = packed.reshape(-1)
+    small_total, loss_sum, count = packed[: small.shape[0]], packed[small.shape[0]], packed[small.shape[0] + 1]
     count = jnp.maximum(count, 1.0)
-    pooled_all = lax.all_gather(pooled_b, ALL, axis=0)
-    logits_all = lax.all_gather(d_logits, ALL, axis=0)
-    own = head_weight.shape[0]
-    first = (lax.axis_index("dp") * lax.axis_size("head") + micro) * own
-    pooled_own = lax.dynamic_slice_in_dim(pooled_all, first, own, 1).astype(jnp.float32)
+    vec_all = vec_all.reshape(-1, 2 * D)
+    rows = head_weight.shape[0]
+    first = (lax.axis_index("dp") * lax.axis_size("head") + micro) * rows
+    pooled_own = lax.dynamic_slice_in_dim(vec_all, first, rows, 1)
     d_head = lax.dot_general(
-        pooled_own, logits_all, (((0,), (0,)), ((), ())), precision=lax.Precision.HIGHEST
-    )
-    d_square = jnp.stack([scatter_rows(d) for d in d_square])
-    grads = (d_square, scatter_rows(d_kv).T, d_head, scatter_rows(d_lat).T, small_total)
+        pooled_own, vec_all[:, D : D + classes], (((0,), (0,)), ((), ())), precision=lax.Precision.HIGHEST
+    )
+    grads = (jnp.stack(own[:10]), own[10][:, :CIN].T, d_head, own[11].T, small_total)
     latent_rate = LATENTS * math.sqrt(D * MICRO * IMG_DEV * lax.axis_size("dp")) / 32.0
     rates = (LEARN_RATE, LEARN_RATE, LEARN_RATE, latent_rate, LEARN_RATE)
     results = [loss_sum, count]
@@ -488,7 +765,7 @@
         P(),
         P(),
     )
-    whole_images = mesh.shape["head"] == MICRO
+    whole_images = dict(mesh.shape) == {"dp": 8, "head": MICRO}
     per_device = per_device_images if whole_images else per_device_rows
     return jax.shard_map(
         per_device, mesh=mesh, in_specs=in_specs, out_specs=out_specs, check_vma=False

time: 2570 us -> 435 us (0.17)
  waiting for transfers between devices: 2200 us -> 0.01 us
  Pallas kernels: 0 us -> 223 us
  blocking collectives: 80.3 us -> 0 us
  matrix products: 149 us -> 104 us
    reduce_scatter x12 -> x0, waiting for transfers between devices: 1530 us -> none  [scatter_rows(): lax.psum_scatter(partial.astype(jnp.bfloat16), ALL, scatter_dimension=0,...]
    all_gather x13 -> x0, waiting for transfers between devices: 662 us -> none  [gather_rows(): return lax.all_gather(shard, ALL, axis=0, tiled=True)]
    pallas_call x0 -> x2, Pallas kernels: none -> 223 us  [the longest x1 114 us: gather_all(): pl.pallas_call(functools.partial(gather_kernel, nt), out_shape=outs, in_s...]
    all_gather x1 -> x0, blocking collectives: 40.7 us -> none  [per_device_images(): pooled_all = lax.all_gather(pooled_b, ALL, axis=0)]
    psum x1 -> x0, blocking collectives: 39.6 us -> none  [per_device_images(): lax.psum((d_small, loss, pick(valid_float)), ALL)]
  transfers between devices with their start and end apart: 27 -> 1, of which waited for: 26 -> 0; matrix products, arithmetic and copies ran while one was open for 6% -> 3% of each run, Pallas kernels for 0% -> 27%
where the time goes in v2:
time: 435 us; the launch traced here: 430 us
  Pallas kernels  223 us (51%)
  matrix products  104 us (24%)
  local copies, waits for them, and re-layouts  52.4 us (12%)
  other arithmetic  39.6 us (9%)
  between operations  6.74 us (2%)
    pallas_call x1, Pallas kernels, gather_all(): pl.pallas_call(functools.partial(gather_kernel, nt), out_shape=outs, in_s...  114 us
    pallas_call x1, Pallas kernels, scatter_all(): pl.pallas_call(functools.partial(scatter_kernel, nt, gap), out_shape=outs...  109 us
    unnamed x251, local copies, waits for them, and re-layouts  36.6 us
    dot_general x11, matrix products, dot_tn(): lax.dot_general(left, right, (((0,), (0,)), ((), ())), preferred_element_...  30.9 us
    dot_general x12, matrix products, dot_nn(): return jnp.dot(left, right, preferred_element_type=jnp.float32)  27.3 us
    dot_general x11, matrix products, dot_nt(): lax.dot_general(left, right, (((1,), (1,)), ((), ())), preferred_element_...  22 us
  transfers between devices with their start and end apart: 1, of which 0 were waited for; matrix products, arithmetic and copies ran while one was open for 3% of the time, Pallas kernels for 27%

profile of v2, /device:TPU:0, one launch (start us, length us, event | category | flops | bytes accessed | tf_op | source)
XLA Modules:
  0.0 430.0 jit_solution(6622779030817692049)
XLA Ops:
  2.4 4.3 %all-to-all-start = ((bf16[4,128,261]{1,2,0:T(8,128)(2,1)}), bf16[4,128,261]{1,2,0:T(8,128)(2,1)S(1)}, u32[]{:S(2)}, u32[]{:S(2)}) async-start(bf16[4,128,261]{1,2,0:T(8,128)(2,1)} %bitcast.258), calls=%async_computation | async-start | bytes 540672 | tf_op jit(solution)/shard_map/all_to_all | solution.py:684
  10.9 114.0 %shard_map.354 = (bf16[4,2,2,2,32,512]{5,4,3,2,1,0:T(8,128)(2,1)}, bf16[4,2,2,2,64,384]{5,4,3,2,1,0:T(8,128)(2,1)}, bf16[4,2,2,2,32,1024]{5,4,3,2,1,0:T(8,128)(2...) custom-call(bf16[32,512]{1,0:T(8,128)(2,1)} %convert_bitcast_fusion., ...), custom_call_target="tpu_custom_call" | custom-call | tf_op jit(solution)/shard_map/pallas_call | solution.py:426
  130.5 2.3 convolution_convert_fusion.19
  141.1 2.6 fusion.100
  147.7 2.8 fusion.99
  156.5 4.5 %convolution_convert_fusion.17 = bf16[512,1024]{1,0:T(8,128)(2,1)} fusion(bf16[512,1024]{1,0:T(8,128)(2,1)} %copy-done.55, bf16[1024,1024]{1,0:T(8,128)(2,1)} %bitcast.315), kind=kOutput, calls=%fused_computation.108 | convolution fusion | flops 1074266112 | bytes 4194304 | tf_op jit(solution)/shard_map/dot_general | solution.py:36
  161.0 2.5 copy.79
  163.6 2.5 multiply_reduce_fusion.1
  173.6 2.6 fusion.98
  180.2 2.8 fusion.97
  188.3 2.7 fusion.72
  195.5 3.4 fusion.14
  208.3 5.0 %multiply_reduce_fusion = (f32[8,512]{1,0:T(8,128)S(1)}, f32[8,512,512]{1,2,0:T(8,128)S(1)}) fusion(f32[8,512,512]{1,2,0:T(8,128)} %copy-done.2, f32[8,512]{1,0:T(8,128)S(1)} %log_add_fusion, bf16[512,8,128]{0,2,1:T(8,128)(2,1)S(1)} %bitcast.261, bf16[64,8,8,128]{3,2,1,0:T(8,128)(2,1)} %copy-done.27), kind=kOutput, calls=%fused_computation.1 | convolution fusion | flops 545255424 | bytes 18907136 | tf_op jit(solution)/shard_map/qhd,khd->hqk/dot_general | solution.py:71
  214.5 2.7 multiply_convert_fusion
  231.5 2.4 fusion.7
  249.8 3.1 fusion.43
  253.0 2.5 convolution_convert_fusion.1
  255.4 3.3 convolution_convert_fusion.2
  258.7 2.8 convolution_convert_fusion.3
  261.6 2.7 convolution_convert_fusion.4
  264.2 3.1 convolution_convert_fusion.5
  267.4 2.7 convolution_convert_fusion.6
  270.1 2.6 convolution_convert_fusion.7
  272.7 2.9 convolution_convert_fusion.8
  275.6 2.8 convolution_convert_fusion.9
  278.4 2.6 convolution_convert_fusion.10
  281.6 2.8 multiply_reduce_fusion.7
  284.4 2.9 convolution_convert_fusion.11
  288.7 2.5 multiply_reduce_fusion.6
  292.6 7.6 %fusion.20 = bf16[1024,512]{0,1:T(8,128)(2,1)S(1)} fusion(f32[512,1024]{1,0:T(8,128)} %get-tuple-element.152, f32[1024,512]{0,1:T(8,128)S(1)} %copy-done.7, f32[512,1024]{1,0:T(8,128)} %get-tuple-element.151, f32[512,1024]{1,0:T(8,128)} %get-tuple-element.148, f32[512,1024]{1,0:T(8,128)} %get-tuple-element.147, f32[512,1024]{1,0:T(8,128)} %get-tuple-element.161, ...), kind=kLoop, calls=%fused_computation.41 | loop fusion | flops 22544384 | bytes 19984384 | tf_op jit(solution)/shard_map/convert_element_type | solution.py:694
  302.2 108.6 %shard_map.355 = (f32[32,1024]{1,0:T(8,128)}, f32[32,1024]{1,0:T(8,128)}, f32[32,1024]{1,0:T(8,128)}, f32[32,1024]{1,0:T(8,128)}, f32[32,1024]{1,0:T(8,128)}, /*...) custom-call(bf16[4,2,2,2,32,1024]{5,4,3,2,1,0:T(8,128)(2,1)} %bitcas, ...), custom_call_target="tpu_custom_call" | custom-call | tf_op jit(solution)/shard_map/pallas_call | solution.py:579
  424.6 2.8 multiply_add_fusion
  (361 shorter events, 107.7 us)
Async XLA Ops:
  0.7 132.7 %copy-start = (s32[4,1]{0,1:T(1,128)S(1)}, s32[4,1]{0,1:T(1,128)}, u32[]{:S(2)}) copy-start(s32[4,1]{0,1:T(1,128)} %param.22) | copy-start | bytes 52
  0.7 8.3 %copy-start.64 = (f32[32,1000]{1,0:T(8,128)S(1)}, f32[32,1000]{1,0:T(8,128)}, u32[]{:S(2)}) copy-start(f32[32,1000]{1,0:T(8,128)} %param.25) | copy-start | bytes 384004
  2.4 6.6 %copy-start.66 = (f32[261,64]{0,1:T(8,128)S(1)}, f32[261,64]{0,1:T(8,128)}, u32[]{:S(2)}) copy-start(f32[261,64]{0,1:T(8,128)} %param.24) | copy-start | bytes 200452
  2.4 7.9 %copy-start.68 = (f32[512,32]{0,1:T(8,128)S(1)}, f32[512,32]{0,1:T(8,128)}, u32[]{:S(2)}) copy-start(f32[512,32]{0,1:T(8,128)} %param.26) | copy-start | bytes 196612
  2.4 132.9 %all-to-all-start = ((bf16[4,128,261]{1,2,0:T(8,128)(2,1)}), bf16[4,128,261]{1,2,0:T(8,128)(2,1)S(1)}, u32[]{:S(2)}, u32[]{:S(2)}) async-start(bf16[4,128,261]{1,2,0:T(8,128)(2,1)} %bitcast.258), calls=%async_computation | async-start | bytes 540672 | tf_op jit(solution)/shard_map/all_to_all | solution.py:684
  128.1 12.3 %copy-start.6 = (f32[1024,512]{0,1:T(8,128)}, f32[1024,512]{0,1:T(8,128)S(1)}, u32[]{:S(2)}) copy-start(f32[1024,512]{0,1:T(8,128)S(1)} %copy.57) | copy-start | bytes 6291460
  132.8 3.8 slice-start.2
  139.6 4.1 copy-start.90
  150.8 4.2 copy-start.83
  156.5 7.0 %copy-start.14 = (bf16[512,1024]{0,1:T(8,128)(2,1)}, bf16[512,1024]{0,1:T(8,128)(2,1)S(1)}, u32[]{:S(2)}) copy-start(bf16[512,1024]{0,1:T(8,128)(2,1)S(1)} %copy.80) | copy-start | bytes 3145732
  166.1 5.5 %copy-start.2 = (f32[8,512,512]{1,2,0:T(8,128)}, f32[8,512,512]{1,2,0:T(8,128)S(1)}, u32[]{:S(2)}) copy-start(f32[8,512,512]{1,2,0:T(8,128)S(1)} %get-tuple-element.150) | copy-start | bytes 25165828
  166.1 4.2 copy-start.56
  188.3 4.9 %copy-start.4 = (f32[512,1024]{1,0:T(8,128)S(1)}, f32[512,1024]{1,0:T(8,128)}, u32[]{:S(2)}) copy-start(f32[512,1024]{1,0:T(8,128)} %copy-done.3) | copy-start | bytes 6291460
  208.3 5.0 %slice-start = ((s8[8388608]{0:T(1024)(128)(4,1)}), s8[4194304]{0:T(1024)(128)(4,1)S(1)}, s32[]{:S(2)}) async-start(s8[8388608]{0:T(1024)(128)(4,1)} %bitcast.259), calls=%async_computation.1 | async-start | bytes 8388608
  208.3 6.2 %slice-start.1 = ((s8[8388608]{0:T(1024)(128)(4,1)}), s8[4194304]{0:T(1024)(128)(4,1)S(1)}, s32[]{:S(2)}) async-start(s8[8388608]{0:T(1024)(128)(4,1)} %bitcast.259), calls=%async_computation.2 | async-start | bytes 8388608
  231.5 6.0 %copy-start.19 = (f32[512,1024]{1,0:T(8,128)}, f32[512,1024]{1,0:T(8,128)S(1)}, u32[]{:S(2)}) copy-start(f32[512,1024]{1,0:T(8,128)S(1)} %add_add_fusion.10) | copy-start | bytes 6291460
  302.2 117.7 %copy-start.81 = (f32[6381]{0:T(1024)S(1)}, f32[6381]{0:T(1024)}, u32[]{:S(2)}) copy-start(f32[6381]{0:T(1024)} %param.37) | copy-start | bytes 76576
  302.2 117.7 %copy-start.82 = (f32[6381]{0:T(1024)S(1)}, f32[6381]{0:T(1024)}, u32[]{:S(2)}) copy-start(f32[6381]{0:T(1024)} %param.32) | copy-start | bytes 76576
  302.2 119.1 %copy-start.79 = (f32[512,32]{0,1:T(8,128)S(1)}, f32[512,32]{0,1:T(8,128)}, u32[]{:S(2)}) copy-start(f32[512,32]{0,1:T(8,128)} %param.36) | copy-start | bytes 196612
  302.2 119.1 %copy-start.80 = (f32[512,32]{0,1:T(8,128)S(1)}, f32[512,32]{0,1:T(8,128)}, u32[]{:S(2)}) copy-start(f32[512,32]{0,1:T(8,128)} %param.31) | copy-start | bytes 196612
  302.2 120.7 %copy-start.78 = (f32[261,64]{0,1:T(8,128)S(1)}, f32[261,64]{0,1:T(8,128)}, u32[]{:S(2)}) copy-start(f32[261,64]{0,1:T(8,128)} %param.29) | copy-start | bytes 200452
  410.8 9.0 %copy-start.75 = (f32[32,1024]{1,0:T(8,128)S(1)}, f32[32,1024]{1,0:T(8,128)}, u32[]{:S(2)}) copy-start(f32[32,1024]{1,0:T(8,128)} %get-tuple-element.69) | copy-start | bytes 393220
  410.8 9.0 %copy-start.74 = (f32[32,1024]{1,0:T(8,128)S(1)}, f32[32,1024]{1,0:T(8,128)}, u32[]{:S(2)}) copy-start(f32[32,1024]{1,0:T(8,128)} %get-tuple-element.70) | copy-start | bytes 393220
  410.8 9.0 %copy-start.73 = (f32[32,1024]{1,0:T(8,128)S(1)}, f32[32,1024]{1,0:T(8,128)}, u32[]{:S(2)}) copy-start(f32[32,1024]{1,0:T(8,128)} %get-tuple-element.71) | copy-start | bytes 393220
  410.8 9.0 %copy-start.72 = (f32[32,1024]{1,0:T(8,128)S(1)}, f32[32,1024]{1,0:T(8,128)}, u32[]{:S(2)}) copy-start(f32[32,1024]{1,0:T(8,128)} %get-tuple-element.72) | copy-start | bytes 393220
  410.8 10.5 %copy-start.69 = (f32[512,32]{0,1:T(8,128)S(1)}, f32[512,32]{0,1:T(8,128)}, u32[]{:S(2)}) copy-start(f32[512,32]{0,1:T(8,128)} %param.26) | copy-start | bytes 196612
  410.9 12.0 %copy-start.67 = (f32[261,64]{0,1:T(8,128)S(1)}, f32[261,64]{0,1:T(8,128)}, u32[]{:S(2)}) copy-start(f32[261,64]{0,1:T(8,128)} %param.24) | copy-start | bytes 200452
  410.9 12.0 %copy-start.77 = (f32[261,64]{0,1:T(8,128)S(1)}, f32[261,64]{0,1:T(8,128)}, u32[]{:S(2)}) copy-start(f32[261,64]{0,1:T(8,128)} %param.34) | copy-start | bytes 200452
  413.3 11.3 %copy-start.26 = (f32[10,32,1024]{2,1,0:T(8,128)S(1)}, f32[10,32,1024]{2,1,0:T(8,128)}, u32[]{:S(2)}) copy-start(f32[10,32,1024]{2,1,0:T(8,128)} %param.23) | copy-start | bytes 3932164
  413.3 11.3 %copy-start.53 = (f32[10,32,1024]{2,1,0:T(8,128)S(1)}, f32[10,32,1024]{2,1,0:T(8,128)}, u32[]{:S(2)}) copy-start(f32[10,32,1024]{2,1,0:T(8,128)} %param.33) | copy-start | bytes 3932164
  413.3 11.3 %copy-start.54 = (f32[10,32,1024]{2,1,0:T(8,128)S(1)}, f32[10,32,1024]{2,1,0:T(8,128)}, u32[]{:S(2)}) copy-start(f32[10,32,1024]{2,1,0:T(8,128)} %param.28) | copy-start | bytes 3932164
  424.6 4.0 copy-start.1
  (89 other events, 207.9 us)
